TPU v7x, 256 devices: a whole 4x4x8 slice. The times are simulated.
256 devices in a mesh: inp: 4 (over z_lo), wt: 8 (over z_hi, y), out: 8 (over x, core).
Axes of the slice: x: 4, y: 4, z: 8 (z_hi: 2, z_lo: 4; z = z_hi * 4 + z_lo), core: 2. Of those that a mesh axis runs over, the one named last changes fastest.
Arguments:
- tokens: bfloat16 [512, 12288], P(('wt', 'out'), 'inp'), may hold values from -6 to 6
- weight_in: bfloat16 [12288, 24576], P('inp', ('wt', 'out')), may hold values from -0.0546875 to 0.0546875
- weight_out: bfloat16 [24576, 12288], P(('wt', 'out'), 'inp'), may hold values from -0.0390625 to 0.0390625
- cotangent: bfloat16 [512, 12288], P(('wt', 'out'), 'inp'), may hold values from -6 to 6
Outputs:
- grad_tokens: bfloat16 [512, 12288], P(('wt', 'out'), 'inp')
- grad_weight_in: bfloat16 [12288, 24576], P('inp', ('wt', 'out'))
- grad_weight_out: bfloat16 [24576, 12288], P(('wt', 'out'), 'inp')
All inputs are finite; a program needn't handle non-finite values.
Results may differ from a plain program's by a relative error of at most 0.02.
Values may be sent and summed in bfloat16 or wider, within the bound.
No kernel may reach another device: no remote copies, remote signals or barrier semaphores. Data moves between devices by JAX's collectives and lax.ppermute only.
A program may use at most 64 MiB of HBM per device.

v0:
```python
import math

import jax
import jax.numpy as jnp
from jax import lax
from jax.sharding import PartitionSpec as P

gelu_scale = math.sqrt(2.0 / math.pi)


def gelu_parts(pre):
    cubic = 0.044715 * pre * pre * pre
    tangent = jnp.tanh(gelu_scale * (pre + cubic))
    gelu_value = 0.5 * pre * (1.0 + tangent)
    gelu_slope = 0.5 * (1.0 + tangent) + 0.5 * pre * (1.0 - tangent * tangent) * gelu_scale * (
        1.0 + 3.0 * 0.044715 * pre * pre
    )
    return (gelu_value, gelu_slope)


def contract(left, right, left_dim, right_dim):
    return lax.dot_general(
        left, right, (((left_dim,), (right_dim,)), ((), ())), preferred_element_type=jnp.float32
    )


def shards(tokens, weight_in, weight_out, cotangent):
    token_full = lax.all_gather(tokens, ("wt", "out"), axis=0, tiled=True)
    cotangent_full = lax.all_gather(cotangent, ("wt", "out"), axis=0, tiled=True)
    row_block = token_full
    pre_rows = lax.psum_scatter(
        jnp.dot(row_block, weight_in, preferred_element_type=jnp.float32).astype(jnp.bfloat16),
        "inp",
        scatter_dimension=0,
        tiled=True,
    ).astype(jnp.float32)
    gelu_value, gelu_slope = gelu_parts(pre_rows)
    act_full = lax.all_gather(gelu_value.astype(jnp.bfloat16), "inp", axis=0, tiled=True)
    row_block = cotangent_full
    grad_act_rows = lax.psum_scatter(
        contract(row_block, weight_out, 1, 1), "inp", scatter_dimension=0, tiled=True
    )
    grad_pre_local = (grad_act_rows * gelu_slope).astype(jnp.bfloat16)
    grad_pre_full = lax.all_gather(grad_pre_local, "inp", axis=0, tiled=True)
    grad_weight_out = contract(act_full, cotangent_full, 0, 0).astype(jnp.bfloat16)
    grad_weight_in = contract(token_full, grad_pre_full, 0, 0).astype(jnp.bfloat16)
    row_block = grad_pre_full
    grad_sum_rows = lax.psum_scatter(
        contract(row_block, weight_in, 1, 1), ("wt", "out"), scatter_dimension=0, tiled=True
    )
    return (grad_sum_rows.astype(jnp.bfloat16), grad_weight_in, grad_weight_out)


def solution(mesh):
    in_specs = (
        P(("wt", "out"), "inp"),
        P("inp", ("wt", "out")),
        P(("wt", "out"), "inp"),
        P(("wt", "out"), "inp"),
    )
    out_specs = (P(("wt", "out"), "inp"), P("inp", ("wt", "out")), P(("wt", "out"), "inp"))
    return jax.shard_map(shards, mesh=mesh, in_specs=in_specs, out_specs=out_specs, check_vma=False)
```

profile of v0, /device:TPU:2, one launch (start us, length us, event | category | flops | bytes accessed | tf_op | source)
XLA Modules:
  0.0 450.4 jit_solution(14147265010918180617)
XLA Ops:
  7.2 0.0 all-gather.5.cloned.1.call-start
  7.2 0.7 all-gather.5.cloned.1.call-update
  7.9 0.0 all-gather.3.cloned.1.call-start
  8.0 0.7 all-gather.3.cloned.1.call-update
  8.7 0.0 reduce-scatter.6.cloned.1.call-start
  8.7 92.4 %all-gather.5.cloned.1.call-done = bf16[512,3072]{1,0:T(8,128)(2,1)} async-done(((bf16[8,3072]{1,0:T(8,128)(2,1)}), bf16[512,3072]{1,0:T(8,128)(2,1)}) %all-gather.5.cloned.1.call-update) | async-done | bytes 3145744 | tf_op jit(solution)/shard_map/all_gather | solution.py:28
  101.1 4.4 convolution_convert_fusion.2
  105.5 0.0 reduce-scatter.6.cloned.1.call-update
  105.5 0.0 reduce-scatter.4.cloned.1.call-start
  105.6 80.6 %all-gather.3.cloned.1.call-done = bf16[512,3072]{1,0:T(8,128)(2,1)} async-done(((bf16[8,3072]{1,0:T(8,128)(2,1)}), bf16[512,3072]{1,0:T(8,128)(2,1)}) %all-gather.3.cloned.1.call-update) | async-done | bytes 3145744 | tf_op jit(solution)/shard_map/all_gather | solution.py:29
  186.2 5.3 %fusion.12 = f32[512,384]{1,0:T(8,128)} fusion(bf16[512,3072]{1,0:T(8,128)(2,1)} %all-gather.3.cloned.1.call-done, bf16[384,3072]{1,0:T(8,128)(2,1)} %param.6), kind=kOutput, calls=%fused_computation.22 | convolution fusion | flops 1207959552 | bytes 6291456 | tf_op jit(solution)/shard_map/dot_general | solution.py:22
  191.5 0.0 reduce-scatter.8.cloned.1.call-start
  191.6 18.7 %reduce-scatter.6.cloned.1.call-done = bf16[128,384]{1,0:T(8,128)(2,1)} async-done(((bf16[512,384]{1,0:T(8,128)(2,1)}), bf16[128,384]{1,0:T(8,128)(2,1)}) %reduce-scatter.6.cloned.1.call-update) | async-done | bytes 98320 | tf_op jit(solution)/shard_map/reduce_scatter | solution.py:31
  210.3 30.2 %reduce-scatter.4.cloned.1.call-done = f32[128,384]{1,0:T(8,128)} async-done(((f32[512,384]{1,0:T(8,128)}), f32[128,384]{1,0:T(8,128)}) %reduce-scatter.4.cloned.1.call-update) | async-done | bytes 196624 | tf_op jit(solution)/shard_map/reduce_scatter | solution.py:40
  240.5 1.1 fusion.8
  241.6 15.0 %all_gather.14 = bf16[512,384]{1,0:T(8,128)(2,1)S(1)} all-gather(bf16[128,384]{1,0:T(8,128)(2,1)S(1)} %get-tuple-element.7), channel_id=1, replica_groups=mesh['inp'=4,'wt'=8,'out'=8] {'inp'}, dimensions={0}, use_global_device_ids=true | all-gather | bytes 491520 | tf_op jit(solution)/shard_map/all_gather | solution.py:44
  256.6 4.5 fusion.13
  261.1 0.0 reduce-scatter.8.cloned.1.call-update
  261.1 4.7 %fusion = bf16[3072,384]{0,1:T(8,128)(2,1)} fusion(bf16[512,384]{1,0:T(8,128)(2,1)S(1)} %all_gather.14, bf16[512,3072]{1,0:T(8,128)(2,1)} %all-gather.5.cloned.1.call-done), kind=kOutput, calls=%fused_computation.2 | convolution fusion | flops 1209139200 | bytes 5898240 | tf_op jit(solution)/shard_map/dot_general | solution.py:22
  265.8 4.3 copy.7
  270.1 14.3 %all_gather.15 = bf16[512,384]{1,0:T(8,128)(2,1)S(1)} all-gather(bf16[128,384]{1,0:T(8,128)(2,1)S(1)} %get-tuple-element.6), channel_id=1, replica_groups=mesh['inp'=4,'wt'=8,'out'=8] {'inp'}, dimensions={0}, use_global_device_ids=true | all-gather | bytes 491520 | tf_op jit(solution)/shard_map/all_gather | solution.py:38
  284.4 4.8 %convolution_convert_fusion = bf16[384,3072]{1,0:T(8,128)(2,1)} fusion(bf16[512,384]{1,0:T(8,128)(2,1)S(1)} %all_gather.15, bf16[512,3072]{1,0:T(8,128)(2,1)} %all-gather.3.cloned.1.call-done), kind=kOutput, calls=%fused_computation | convolution fusion | flops 1209139200 | bytes 5898240 | tf_op jit(solution)/shard_map/dot_general | solution.py:22
  289.2 153.2 %reduce-scatter.8.cloned.1.call-done = f32[8,3072]{1,0:T(8,128)} async-done(((f32[512,3072]{1,0:T(8,128)}), f32[8,3072]{1,0:T(8,128)}) %reduce-scatter.8.cloned.1.call-update) | async-done | bytes 98320 | tf_op jit(solution)/shard_map/reduce_scatter | solution.py:48
  442.4 1.5 convert_element_type.27
  (3 shorter events, 0.0 us)
Async XLA Ops:
  7.2 93.9 %copy-start = (bf16[3072,384]{1,0:T(8,128)(2,1)S(1)}, bf16[3072,384]{1,0:T(8,128)(2,1)}, u32[]{:S(2)}) copy-start(bf16[3072,384]{1,0:T(8,128)(2,1)} %param.5) | copy-start | bytes 7077892
  7.2 93.9 %all-gather.5.cloned.1.call-start = ((), (), s32[]{:S(2)}) async-start(), calls=%async_computation.5 | async-start | bytes 3194880 | tf_op jit(solution)/shard_map/all_gather | solution.py:28
  7.9 178.3 %all-gather.3.cloned.1.call-start = ((), (), s32[]{:S(2)}) async-start(), calls=%async_computation.3 | async-start | bytes 3194880 | tf_op jit(solution)/shard_map/all_gather | solution.py:29
  8.7 201.6 %reduce-scatter.6.cloned.1.call-start = ((), (), s32[]{:S(2)}) async-start(), calls=%async_computation.6 | async-start | bytes 491520 | tf_op jit(solution)/shard_map/reduce_scatter | solution.py:31
  105.5 135.0 %reduce-scatter.4.cloned.1.call-start = ((), (), s32[]{:S(2)}) async-start(), calls=%async_computation.4 | async-start | bytes 983040 | tf_op jit(solution)/shard_map/reduce_scatter | solution.py:40
  191.5 250.9 %reduce-scatter.8.cloned.1.call-start = ((), (), s32[]{:S(2)}) async-start(), calls=%async_computation.7 | async-start | bytes 6389760 | tf_op jit(solution)/shard_map/reduce_scatter | solution.py:48
Sparse Core Ops, SparseCore 0:
  11.7 89.2 all-gather.4
  104.8 81.3 all-gather.2
  189.3 20.9 reduce-scatter.5
  213.4 27.0 reduce-scatter.3
  261.2 181.0 reduce-scatter.7
where the time goes:
time: 451 us; the launch traced here: 450 us
  waiting for transfers between devices  377 us (84%)
  blocking collectives  29.3 us (6%)
  matrix products  23.7 us (5%)
  between operations  13.8 us (3%)
    reduce_scatter x1, waiting for transfers between devices, shards(): lax.psum_scatter(contract(row_block, weight_in, 1, 1), ('wt', 'out'), sca...  153 us
    all_gather x1, waiting for transfers between devices, shards(): token_full = lax.all_gather(tokens, ('wt', 'out'), axis=0, tiled=True)  92.4 us
    all_gather x1, waiting for transfers between devices, shards(): lax.all_gather(cotangent, ('wt', 'out'), axis=0, tiled=True)  80.6 us
    reduce_scatter x1, waiting for transfers between devices, shards(): lax.psum_scatter(contract(row_block, weight_out, 1, 1), 'inp', scatter_di...  30.2 us
    dot_general x4, matrix products, contract(): lax.dot_general(left, right, (((left_dim,), (right_dim,)), ((), ())), pre...  19.3 us
    reduce_scatter x1, waiting for transfers between devices, shards(): lax.psum_scatter(jnp.dot(row_block, weight_in, preferred_element_type=jnp...  18.7 us
    all_gather x1, blocking collectives, shards(): grad_pre_full = lax.all_gather(grad_pre_local, 'inp', axis=0, tiled=True)  15 us
    all_gather x1, blocking collectives, shards(): lax.all_gather(gelu_value.astype(jnp.bfloat16), 'inp', axis=0, tiled=True)  14.3 us
  transfers between devices with their start and end apart: 5, of which 5 were waited for; matrix products, arithmetic and copies ran while one was open for 5% of the time, Pallas kernels for 0%

commit v1 on v0

v1 whole, which is shorter than its diff:
```python
import math

import jax
import jax.numpy as jnp
from jax import lax
from jax.sharding import PartitionSpec as P

gelu_scale = math.sqrt(2.0 / math.pi)
bf16, f32 = jnp.bfloat16, jnp.float32


def gelu_parts(pre):
    cubic = 0.044715 * pre * pre * pre
    tangent = jnp.tanh(gelu_scale * (pre + cubic))
    gelu_value = 0.5 * pre * (1.0 + tangent)
    gelu_slope = 0.5 * (1.0 + tangent) + 0.5 * pre * (1.0 - tangent * tangent) * gelu_scale * (
        1.0 + 3.0 * 0.044715 * pre * pre
    )
    return (gelu_value, gelu_slope)


def contract(left, right, left_dim, right_dim):
    return lax.dot_general(
        left, right, (((left_dim,), (right_dim,)), ((), ())), preferred_element_type=f32
    )


def even_pair(place):
    return place ^ 1


def odd_pair(place):
    return (place + 1) % 4 if place % 2 else (place - 1) % 4


def swap(value, partner):
    pairs = []
    for z in range(2):
        for y in range(4):
            for x in range(4):
                for core in range(2):
                    pz, py, px, pc = partner(z, y, x, core)
                    pairs.append(((z * 4 + y) * 8 + x * 2 + core, (pz * 4 + py) * 8 + px * 2 + pc))
    return lax.ppermute(value, ("wt", "out"), pairs)


def swap_z(value):
    return swap(value, lambda z, y, x, core: (1 - z, y, x, core))


def swap_core(value):
    return swap(value, lambda z, y, x, core: (z, y, x, 1 - core))


ORDERS = (
    (("x", even_pair), ("x", odd_pair), ("y", even_pair), ("y", odd_pair)),
    (("x", odd_pair), ("x", even_pair), ("y", odd_pair), ("y", even_pair)),
)


def swap_chip(value, chunk, step):
    orders = (ORDERS[chunk], ORDERS[chunk][2:] + ORDERS[chunk][:2])

    def partner(z, y, x, core):
        axis, pair = orders[core][step]
        return (z, pair(y), x, core) if axis == "y" else (z, y, pair(x), core)

    return swap(value, partner)


def move_inp(value, step):
    return lax.ppermute(value, "inp", [(i, (i + step) % 4) for i in range(4)])


def gather_chips(value, chunk):
    for step in range(4):
        value = jnp.concatenate([value, swap_chip(value, chunk, step)], 0)
    return value


def sum_chips(total, chunk):
    for step in (3, 2, 1, 0):
        rows = total.shape[0] // 2
        total = total[:rows] + swap_chip(total[rows:].astype(bf16), chunk, step).astype(f32)
    return total


def sum_inp(partial):
    me = lax.axis_index("inp")
    rows = partial.shape[0] // 4
    block = lambda step: lax.dynamic_slice_in_dim(partial, (me + step) % 4 * rows, rows, 0)
    total = block(0).astype(f32)
    for step in (1, 2, 3):
        total = total + move_inp(block(step), step).astype(f32)
    return total


def gather_inp(value):
    me = lax.axis_index("inp")
    rows = value.shape[0]
    full = jnp.zeros((4 * rows, value.shape[1]), value.dtype)
    full = lax.dynamic_update_slice_in_dim(full, value, me * rows, 0)
    for step in (1, 2, 3):
        full = lax.dynamic_update_slice_in_dim(full, move_inp(value, -step), (me + step) % 4 * rows, 0)
    return full


def shards(tokens, weight_in, weight_out, cotangent):
    own = jnp.concatenate([tokens, cotangent], 1)
    chunks = (own, swap_z(own))
    token_rows, cotangent_rows, act, grad_pre, sums = [], [], [], [], []
    partials = []
    for chunk in range(2):
        own = gather_chips(chunks[chunk], chunk)
        pieces = (own, swap_core(own))
        token_rows += [piece[:, :3072] for piece in pieces]
        cotangent_rows += [piece[:, 3072:] for piece in pieces]
        partials.append(
            jnp.concatenate(
                [
                    jnp.concatenate(
                        [
                            jnp.dot(piece[:, :3072], weight_in, preferred_element_type=f32).astype(bf16),
                            contract(piece[:, 3072:], weight_out, 1, 1).astype(bf16),
                        ],
                        1,
                    )
                    for piece in pieces
                ],
                0,
            )
        )
    for chunk in range(2):
        rows = sum_inp(partials[chunk])
        gelu_value, gelu_slope = gelu_parts(rows[:, :384])
        rows = jnp.concatenate([gelu_value, rows[:, 384:] * gelu_slope], 1).astype(bf16)
        rows = gather_inp(rows)
        act.append(rows[:, :384])
        grad_pre.append(rows[:, 384:])
        sums.append(contract(rows[:, 384:], weight_in, 1, 1))
    totals = []
    for chunk in range(2):
        total = sums[chunk][:128] + swap_core(sums[chunk][128:].astype(bf16)).astype(f32)
        totals.append(sum_chips(total, chunk))
    grad_tokens = totals[0] + swap_z(totals[1].astype(bf16)).astype(f32)
    grad_weight_in = contract(jnp.concatenate(token_rows, 0), jnp.concatenate(grad_pre, 0), 0, 0)
    grad_weight_out = contract(jnp.concatenate(act, 0), jnp.concatenate(cotangent_rows, 0), 0, 0)
    return (grad_tokens.astype(bf16), grad_weight_in.astype(bf16), grad_weight_out.astype(bf16))


def solution(mesh):
    in_specs = (
        P(("wt", "out"), "inp"),
        P("inp", ("wt", "out")),
        P(("wt", "out"), "inp"),
        P(("wt", "out"), "inp"),
    )
    out_specs = (P(("wt", "out"), "inp"), P("inp", ("wt", "out")), P(("wt", "out"), "inp"))
    return jax.shard_map(shards, mesh=mesh, in_specs=in_specs, out_specs=out_specs, check_vma=False)
```

time: 451 us -> 137 us (0.30)
  waiting for transfers between devices: 377 us -> 42.9 us
  starting transfers between devices: 0.2 us -> 63.8 us
  blocking collectives: 29.3 us -> 0 us
  between operations: 13.8 us -> 1.17 us
  matrix products: 23.7 us -> 15.8 us
    reduce_scatter x3 -> x0, waiting for transfers between devices: 202 us -> none  [the longest x1 153 us: shards(): lax.psum_scatter(contract(row_block, weight_in, 1, 1), ('wt', 'out'), sca...]
    all_gather x2 -> x0, waiting for transfers between devices: 173 us -> none  [the longest x1 92.4 us: shards(): token_full = lax.all_gather(tokens, ('wt', 'out'), axis=0, tiled=True)]
    ppermute x0 -> x34, starting transfers between devices: none -> 63.8 us  [the longest x22 37.2 us: swap(): return lax.ppermute(value, ('wt', 'out'), pairs)]
    ppermute x0 -> x34, waiting for transfers between devices: none -> 42.9 us  [the longest x22 32.7 us: swap(): return lax.ppermute(value, ('wt', 'out'), pairs)]
    all_gather x2 -> x0, blocking collectives: 29.3 us -> none  [the longest x1 15 us: shards(): grad_pre_full = lax.all_gather(grad_pre_local, 'inp', axis=0, tiled=True)]
    dot_general x4 -> x8, matrix products: 19.3 us -> 12.2 us  [contract(): lax.dot_general(left, right, (((left_dim,), (right_dim,)), ((), ())), pre...]
  transfers between devices with their start and end apart: 5 -> 34, of which waited for: 5 -> 16; matrix products, arithmetic and copies ran while one was open for 5% -> 16% of each run, Pallas kernels for 0% -> 0%
where the time goes in v1:
time: 137 us; the launch traced here: 134 us
  starting transfers between devices  63.8 us (47%)
  waiting for transfers between devices  42.9 us (31%)
  matrix products  15.8 us (12%)
  local copies, waits for them, and re-layouts  8.6 us (6%)
  other arithmetic  1.77 us (1%)
    ppermute x22, starting transfers between devices, swap(): return lax.ppermute(value, ('wt', 'out'), pairs)  37.2 us
    ppermute x22, waiting for transfers between devices, swap(): return lax.ppermute(value, ('wt', 'out'), pairs)  32.7 us
    ppermute x12, starting transfers between devices, move_inp(): return lax.ppermute(value, 'inp', [(i, (i + step) % 4) for i in range(4)])  26.6 us
    dot_general x8, matrix products, contract(): lax.dot_general(left, right, (((left_dim,), (right_dim,)), ((), ())), pre...  12.2 us
    ppermute x12, waiting for transfers between devices, move_inp(): return lax.ppermute(value, 'inp', [(i, (i + step) % 4) for i in range(4)])  10.2 us
    unnamed x12, local copies, waits for them, and re-layouts  3.75 us
    dot_general x4, matrix products, shards(): jnp.dot(piece[:, :3072], weight_in, preferred_element_type=f32).astype(bf16)  3.57 us
  transfers between devices with their start and end apart: 34, of which 16 were waited for; matrix products, arithmetic and copies ran while one was open for 16% of the time, Pallas kernels for 0%

profile of v1, /device:TPU:2, one launch (start us, length us, event | category | flops | bytes accessed | tf_op | source)
XLA Modules:
  0.0 134.0 jit_solution(6718861809707832437)
XLA Ops:
  3.6 2.3 %collective-permute-start = (bf16[8,6144]{1,0:T(8,128)(2,1)S(1)}, bf16[8,6144]{1,0:T(8,128)(2,1)S(1)}, u32[]{:S(2)}, u32[]{:S(2)}) collective-permute-start(bf16[8,6144]{1,0:T(8,128)(2,1)S(1)} %get-tuple-element.29), channel_id=1, source_target_pairs={{0,2},{1,9},{2,0},{3,11},{4,6},{5,13},{6,4},{7,15},{8,10},{9,1},{1... | collective-permute-start | bytes 294920 | tf_op jit(solution)/shard_map/ppermute | solution.py:44
  5.9 5.5 %collective-permute-start.16 = (bf16[8,6144]{1,0:T(8,128)(2,1)S(1)}, bf16[8,6144]{1,0:T(8,128)(2,1)S(1)}, u32[]{:S(2)}, u32[]{:S(2)}) collective-permute-start(bf16[8,6144]{1,0:T(8,128)(2,1)S(1)} %get-tuple-element.29), channel_id=1, source_target_pairs={{0,32},{1,33},{2,34},{3,35},{4,36},{5,37},{6,38},{7,39},{8,40},{9,... | collective-permute-start | bytes 294920 | tf_op jit(solution)/shard_map/ppermute | solution.py:44
  11.4 2.2 %collective-permute-start.1 = (bf16[16,6144]{1,0:T(8,128)(2,1)S(1)}, bf16[16,6144]{1,0:T(8,128)(2,1)S(1)}, u32[]{:S(2)}, u32[]{:S(2)}) collective-permute-start(bf16[16,6144]{1,0:T(8,128)(2,1)S(1)} %pad_maximum_fusion.4), channel_id=1, source_target_pairs={{0,6},{1,25},{2,4},{3,27},{4,2},{5,29},{6,0},{7,31},{8,14},{9,17},... | collective-permute-start | bytes 589832 | tf_op jit(solution)/shard_map/ppermute | solution.py:44
  17.2 2.5 %collective-permute-done.17 = bf16[8,6144]{1,0:T(8,128)(2,1)S(1)} collective-permute-done((bf16[8,6144]{1,0:T(8,128)(2,1)S(1)}, bf16[8,6144]{1,0:T(8,128)(2,1)S(1)}, u32[]{:S(2)}, u32[]{:S(2)}) %collective-permute-start.17) | collective-permute-done | bytes 98336 | tf_op jit(solution)/shard_map/ppermute | solution.py:44
  19.7 2.7 %collective-permute-start.18 = (bf16[16,6144]{1,0:T(8,128)(2,1)S(1)}, bf16[16,6144]{1,0:T(8,128)(2,1)S(1)}, u32[]{:S(2)}, u32[]{:S(2)}) collective-permute-start(bf16[16,6144]{1,0:T(8,128)(2,1)S(1)} %pad_maximum_fusion.5), channel_id=1, source_target_pairs={{0,2},{1,9},{2,0},{3,11},{4,6},{5,13},{6,4},{7,15},{8,10},{9,1},{1... | collective-permute-start | bytes 589832 | tf_op jit(solution)/shard_map/ppermute | solution.py:44
  24.0 4.2 %collective-permute-done.18 = bf16[16,6144]{1,0:T(8,128)(2,1)S(1)} collective-permute-done((bf16[16,6144]{1,0:T(8,128)(2,1)S(1)}, bf16[16,6144]{1,0:T(8,128)(2,1)S(1)}, u32[]{:S(2)}, u32[]{:S(2)}) %collective-permute-start.18) | collective-permute-done | bytes 196640 | tf_op jit(solution)/shard_map/ppermute | solution.py:44
  28.2 2.4 %collective-permute-start.19 = (bf16[32,6144]{1,0:T(8,128)(2,1)S(1)}, bf16[32,6144]{1,0:T(8,128)(2,1)S(1)}, u32[]{:S(2)}, u32[]{:S(2)}) collective-permute-start(bf16[32,6144]{1,0:T(8,128)(2,1)S(1)} %pad_maximum_fusion.3), channel_id=1, source_target_pairs={{0,24},{1,7},{2,26},{3,5},{4,28},{5,3},{6,30},{7,1},{8,16},{9,15},... | collective-permute-start | bytes 1179656 | tf_op jit(solution)/shard_map/ppermute | solution.py:44
  33.4 3.9 %collective-permute-done.19 = bf16[32,6144]{1,0:T(8,128)(2,1)S(1)} collective-permute-done((bf16[32,6144]{1,0:T(8,128)(2,1)S(1)}, bf16[32,6144]{1,0:T(8,128)(2,1)S(1)}, u32[]{:S(2)}, u32[]{:S(2)}) %collective-permute-start.19) | collective-permute-done | bytes 393248 | tf_op jit(solution)/shard_map/ppermute | solution.py:44
  37.5 8.2 %collective-permute-done.3 = bf16[64,6144]{1,0:T(8,128)(2,1)S(1)} collective-permute-done((bf16[64,6144]{1,0:T(8,128)(2,1)S(1)}, bf16[64,6144]{1,0:T(8,128)(2,1)S(1)}, u32[]{:S(2)}, u32[]{:S(2)}) %collective-permute-start.3) | collective-permute-done | bytes 786464 | tf_op jit(solution)/shard_map/ppermute | solution.py:44
  62.8 3.7 %collective-permute-start.24 = (bf16[64,768]{1,0:T(8,128)(2,1)S(1)}, bf16[64,768]{1,0:T(8,128)(2,1)S(1)}, u32[]{:S(2)}, u32[]{:S(2)}) collective-permute-start(bf16[64,768]{1,0:T(8,128)(2,1)S(1)} %get-tuple-element.16), channel_id=1, source_target_pairs={{0,192},{64,0},{128,64},{192,128},{1,193},{65,1},{129,65},{193,129... | collective-permute-start | bytes 294920 | tf_op jit(solution)/shard_map/ppermute | solution.py:72
  66.5 2.2 %collective-permute-start.23 = (bf16[64,768]{1,0:T(8,128)(2,1)S(1)}, bf16[64,768]{1,0:T(8,128)(2,1)S(1)}, u32[]{:S(2)}, u32[]{:S(2)}) collective-permute-start(bf16[64,768]{1,0:T(8,128)(2,1)S(1)} %get-tuple-element.17), channel_id=1, source_target_pairs={{0,128},{64,192},{128,0},{192,64},{1,129},{65,193},{129,1},{193,65... | collective-permute-start | bytes 294920 | tf_op jit(solution)/shard_map/ppermute | solution.py:72
  68.8 4.6 %collective-permute-done.6 = bf16[64,768]{1,0:T(8,128)(2,1)S(1)} collective-permute-done((bf16[64,768]{1,0:T(8,128)(2,1)S(1)}, bf16[64,768]{1,0:T(8,128)(2,1)S(1)}, u32[]{:S(2)}, u32[]{:S(2)}) %collective-permute-start.6) | collective-permute-done | bytes 98336 | tf_op jit(solution)/shard_map/ppermute | solution.py:72
  73.4 3.6 %collective-permute-done.23 = bf16[64,768]{1,0:T(8,128)(2,1)S(1)} collective-permute-done((bf16[64,768]{1,0:T(8,128)(2,1)S(1)}, bf16[64,768]{1,0:T(8,128)(2,1)S(1)}, u32[]{:S(2)}, u32[]{:S(2)}) %collective-permute-start.23) | collective-permute-done | bytes 98336 | tf_op jit(solution)/shard_map/ppermute | solution.py:72
  77.5 2.2 %collective-permute-start.8 = (bf16[64,768]{1,0:T(8,128)(2,1)S(1)}, bf16[64,768]{1,0:T(8,128)(2,1)S(1)}, u32[]{:S(2)}, u32[]{:S(2)}) collective-permute-start(bf16[64,768]{1,0:T(8,128)(2,1)S(1)} %get-tuple-element.27), channel_id=1, source_target_pairs={{0,192},{64,0},{128,64},{192,128},{1,193},{65,1},{129,65},{193,129... | collective-permute-start | bytes 294920 | tf_op jit(solution)/shard_map/ppermute | solution.py:72
  80.3 2.2 %collective-permute-start.26 = (bf16[64,768]{1,0:T(8,128)(2,1)S(1)}, bf16[64,768]{1,0:T(8,128)(2,1)S(1)}, u32[]{:S(2)}, u32[]{:S(2)}) collective-permute-start(bf16[64,768]{1,0:T(8,128)(2,1)S(1)} %get-tuple-element.25), channel_id=1, source_target_pairs={{0,128},{64,192},{128,0},{192,64},{1,129},{65,193},{129,1},{193,65... | collective-permute-start | bytes 294920 | tf_op jit(solution)/shard_map/ppermute | solution.py:72
  82.5 2.3 %collective-permute-start.25 = (bf16[64,768]{1,0:T(8,128)(2,1)S(1)}, bf16[64,768]{1,0:T(8,128)(2,1)S(1)}, u32[]{:S(2)}, u32[]{:S(2)}) collective-permute-start(bf16[64,768]{1,0:T(8,128)(2,1)S(1)} %get-tuple-element.25), channel_id=1, source_target_pairs={{0,192},{64,0},{128,64},{192,128},{1,193},{65,1},{129,65},{193,129... | collective-permute-start | bytes 294920 | tf_op jit(solution)/shard_map/ppermute | solution.py:72
  85.7 7.8 %collective-permute-start.27 = (bf16[64,768]{1,0:T(8,128)(2,1)S(1)}, bf16[64,768]{1,0:T(8,128)(2,1)S(1)}, u32[]{:S(2)}, u32[]{:S(2)}) collective-permute-start(bf16[64,768]{1,0:T(8,128)(2,1)S(1)} %get-tuple-element.25), channel_id=1, source_target_pairs={{0,64},{64,128},{128,192},{192,0},{1,65},{65,129},{129,193},{193,1... | collective-permute-start | bytes 294920 | tf_op jit(solution)/shard_map/ppermute | solution.py:72
  97.8 3.1 %convolution_convert_fusion.1 = bf16[3072,384]{1,0:T(8,128)(2,1)} fusion(bf16[128,3072]{1,0:T(8,128)(2,1)S(1)} %get-tuple-element.10, bf16[128,3072]{1,0:T(8,128)(2,1)S(1)} %get-tuple-element.8, bf16[128,3072]{1,0:T(8,128)(2,1)S(1)} %get-tuple-element.6, bf16[128,3072]{1,0:T(8,128)(2,1)S(1)} %get-tuple-element.4, ...), kind=kOutput, calls=%fused_computation.1 | convolution fusion | flops 1222508544 | bytes 5898240 | tf_op jit(solution)/shard_map/dot_general | solution.py:23
  101.6 2.3 %collective-permute-start.12 = (bf16[64,3072]{1,0:T(8,128)(2,1)S(1)}, bf16[64,3072]{1,0:T(8,128)(2,1)S(1)}, u32[]{:S(2)}, u32[]{:S(2)}) collective-permute-start(bf16[64,3072]{1,0:T(8,128)(2,1)S(1)} %slice.265), channel_id=1, source_target_pairs={{0,24},{1,7},{2,26},{3,5},{4,28},{5,3},{6,30},{7,1},{8,16},{9,15},... | collective-permute-start | bytes 1179656 | tf_op jit(solution)/shard_map/ppermute | solution.py:44
  104.0 5.2 %collective-permute-done.29 = bf16[64,3072]{1,0:T(8,128)(2,1)S(1)} collective-permute-done((bf16[64,3072]{1,0:T(8,128)(2,1)S(1)}, bf16[64,3072]{1,0:T(8,128)(2,1)S(1)}, u32[]{:S(2)}, u32[]{:S(2)}) %collective-permute-start.29) | collective-permute-done | bytes 393248 | tf_op jit(solution)/shard_map/ppermute | solution.py:44
  109.3 2.2 %collective-permute-start.30 = (bf16[32,3072]{1,0:T(8,128)(2,1)S(1)}, bf16[32,3072]{1,0:T(8,128)(2,1)S(1)}, u32[]{:S(2)}, u32[]{:S(2)}) collective-permute-start(bf16[32,3072]{1,0:T(8,128)(2,1)S(1)} %slice.266), channel_id=1, source_target_pairs={{0,24},{1,7},{2,26},{3,5},{4,28},{5,3},{6,30},{7,1},{8,16},{9,15},... | collective-permute-start | bytes 589832 | tf_op jit(solution)/shard_map/ppermute | solution.py:44
  111.8 4.5 %collective-permute-done.30 = bf16[32,3072]{1,0:T(8,128)(2,1)S(1)} collective-permute-done((bf16[32,3072]{1,0:T(8,128)(2,1)S(1)}, bf16[32,3072]{1,0:T(8,128)(2,1)S(1)}, u32[]{:S(2)}, u32[]{:S(2)}) %collective-permute-start.30) | collective-permute-done | bytes 196640 | tf_op jit(solution)/shard_map/ppermute | solution.py:44
  125.3 5.4 %collective-permute-start.33 = (bf16[8,3072]{1,0:T(8,128)(2,1)S(1)}, bf16[8,3072]{1,0:T(8,128)(2,1)S(1)}, u32[]{:S(2)}, u32[]{:S(2)}) collective-permute-start(bf16[8,3072]{1,0:T(8,128)(2,1)S(1)} %fusion.34), channel_id=1, source_target_pairs={{0,32},{1,33},{2,34},{3,35},{4,36},{5,37},{6,38},{7,39},{8,40},{9,... | collective-permute-start | bytes 147464 | tf_op jit(solution)/shard_map/ppermute | solution.py:44
  130.7 2.6 %convolution_convert_fusion = bf16[384,3072]{1,0:T(8,128)(2,1)} fusion(bf16[128,3072]{1,0:T(8,128)(2,1)S(1)} %get-tuple-element.9, bf16[128,3072]{1,0:T(8,128)(2,1)S(1)} %get-tuple-element.7, bf16[128,3072]{1,0:T(8,128)(2,1)S(1)} %get-tuple-element.5, bf16[128,3072]{1,0:T(8,128)(2,1)S(1)} %get-tuple-element.3, bf16[256,384]{1,0:T(8,128)(2,1)S(1)} %get-tuple-element.13, ...), kind=kOutput, calls=%fused_computation | convolution fusion | flops 1222508544 | bytes 5898240 | tf_op jit(solution)/shard_map/dot_general | solution.py:23
  (120 shorter events, 45.0 us)
Async XLA Ops:
  5.9 9.1 %collective-permute-start.16 = (bf16[8,6144]{1,0:T(8,128)(2,1)S(1)}, bf16[8,6144]{1,0:T(8,128)(2,1)S(1)}, u32[]{:S(2)}, u32[]{:S(2)}) collective-permute-start(bf16[8,6144]{1,0:T(8,128)(2,1)S(1)} %get-tuple-element.29), channel_id=1, source_target_pairs={{0,32},{1,33},{2,34},{3,35},{4,36},{5,37},{6,38},{7,39},{8,40},{9,... | collective-permute-start | bytes 294920 | tf_op jit(solution)/shard_map/ppermute | solution.py:44
  11.4 11.0 %collective-permute-start.1 = (bf16[16,6144]{1,0:T(8,128)(2,1)S(1)}, bf16[16,6144]{1,0:T(8,128)(2,1)S(1)}, u32[]{:S(2)}, u32[]{:S(2)}) collective-permute-start(bf16[16,6144]{1,0:T(8,128)(2,1)S(1)} %pad_maximum_fusion.4), channel_id=1, source_target_pairs={{0,6},{1,25},{2,4},{3,27},{4,2},{5,29},{6,0},{7,31},{8,14},{9,17},... | collective-permute-start | bytes 589832 | tf_op jit(solution)/shard_map/ppermute | solution.py:44
  19.7 8.5 %collective-permute-start.18 = (bf16[16,6144]{1,0:T(8,128)(2,1)S(1)}, bf16[16,6144]{1,0:T(8,128)(2,1)S(1)}, u32[]{:S(2)}, u32[]{:S(2)}) collective-permute-start(bf16[16,6144]{1,0:T(8,128)(2,1)S(1)} %pad_maximum_fusion.5), channel_id=1, source_target_pairs={{0,2},{1,9},{2,0},{3,11},{4,6},{5,13},{6,4},{7,15},{8,10},{9,1},{1... | collective-permute-start | bytes 589832 | tf_op jit(solution)/shard_map/ppermute | solution.py:44
  22.4 8.2 %collective-permute-start.2 = (bf16[32,6144]{1,0:T(8,128)(2,1)S(1)}, bf16[32,6144]{1,0:T(8,128)(2,1)S(1)}, u32[]{:S(2)}, u32[]{:S(2)}) collective-permute-start(bf16[32,6144]{1,0:T(8,128)(2,1)S(1)} %pad_maximum_fusion.2), channel_id=1, source_target_pairs={{0,8},{1,3},{2,10},{3,1},{4,12},{5,7},{6,14},{7,5},{8,0},{9,11},{1... | collective-permute-start | bytes 1179656 | tf_op jit(solution)/shard_map/ppermute | solution.py:44
  28.2 9.1 %collective-permute-start.19 = (bf16[32,6144]{1,0:T(8,128)(2,1)S(1)}, bf16[32,6144]{1,0:T(8,128)(2,1)S(1)}, u32[]{:S(2)}, u32[]{:S(2)}) collective-permute-start(bf16[32,6144]{1,0:T(8,128)(2,1)S(1)} %pad_maximum_fusion.3), channel_id=1, source_target_pairs={{0,24},{1,7},{2,26},{3,5},{4,28},{5,3},{6,30},{7,1},{8,16},{9,15},... | collective-permute-start | bytes 1179656 | tf_op jit(solution)/shard_map/ppermute | solution.py:44
  30.7 15.0 %collective-permute-start.3 = (bf16[64,6144]{1,0:T(8,128)(2,1)S(1)}, bf16[64,6144]{1,0:T(8,128)(2,1)S(1)}, u32[]{:S(2)}, u32[]{:S(2)}) collective-permute-start(bf16[64,6144]{1,0:T(8,128)(2,1)S(1)} %pad_maximum_fusion), channel_id=1, source_target_pairs={{0,24},{1,7},{2,26},{3,5},{4,28},{5,3},{6,30},{7,1},{8,16},{9,15},... | collective-permute-start | bytes 2359304 | tf_op jit(solution)/shard_map/ppermute | solution.py:44
  37.3 14.5 %collective-permute-start.20 = (bf16[64,6144]{1,0:T(8,128)(2,1)S(1)}, bf16[64,6144]{1,0:T(8,128)(2,1)S(1)}, u32[]{:S(2)}, u32[]{:S(2)}) collective-permute-start(bf16[64,6144]{1,0:T(8,128)(2,1)S(1)} %pad_maximum_fusion.1), channel_id=1, source_target_pairs={{0,8},{1,3},{2,10},{3,1},{4,12},{5,7},{6,14},{7,5},{8,0},{9,11},{1... | collective-permute-start | bytes 2359304 | tf_op jit(solution)/shard_map/ppermute | solution.py:44
  51.9 9.2 %collective-permute-start.21 = (bf16[128,6144]{1,0:T(8,128)(2,1)S(1)}, bf16[128,6144]{1,0:T(8,128)(2,1)S(1)}, u32[]{:S(2)}, u32[]{:S(2)}) collective-permute-start(bf16[128,6144]{1,0:T(8,128)(2,1)S(1)} %constant_dynamic-update-slice_fusion.8), channel_id=1, source_target_pairs={{0,1},{1,0},{2,3},{3,2},{4,5},{5,4},{6,7},{7,6},{8,9},{9,8},{10,11... | collective-permute-start | bytes 4718600 | tf_op jit(solution)/shard_map/ppermute | solution.py:44
  55.6 10.9 %collective-permute-start.5 = (bf16[64,768]{1,0:T(8,128)(2,1)S(1)}, bf16[64,768]{1,0:T(8,128)(2,1)S(1)}, u32[]{:S(2)}, u32[]{:S(2)}) collective-permute-start(bf16[64,768]{1,0:T(8,128)(2,1)S(1)} %get-tuple-element.18), channel_id=1, source_target_pairs={{0,64},{64,128},{128,192},{192,0},{1,65},{65,129},{129,193},{193,1... | collective-permute-start | bytes 294920 | tf_op jit(solution)/shard_map/ppermute | solution.py:72
  57.3 11.5 %collective-permute-start.7 = (bf16[64,768]{1,0:T(8,128)(2,1)S(1)}, bf16[64,768]{1,0:T(8,128)(2,1)S(1)}, u32[]{:S(2)}, u32[]{:S(2)}) collective-permute-start(bf16[64,768]{1,0:T(8,128)(2,1)S(1)} %get-tuple-element.19), channel_id=1, source_target_pairs={{0,192},{64,0},{128,64},{192,128},{1,193},{65,1},{129,65},{193,129... | collective-permute-start | bytes 294920 | tf_op jit(solution)/shard_map/ppermute | solution.py:72
  59.5 13.9 %collective-permute-start.6 = (bf16[64,768]{1,0:T(8,128)(2,1)S(1)}, bf16[64,768]{1,0:T(8,128)(2,1)S(1)}, u32[]{:S(2)}, u32[]{:S(2)}) collective-permute-start(bf16[64,768]{1,0:T(8,128)(2,1)S(1)} %get-tuple-element.20), channel_id=1, source_target_pairs={{0,128},{64,192},{128,0},{192,64},{1,129},{65,193},{129,1},{193,65... | collective-permute-start | bytes 294920 | tf_op jit(solution)/shard_map/ppermute | solution.py:72
  62.6 10.8 %collective-permute-start.22 = (bf16[64,768]{1,0:T(8,128)(2,1)S(1)}, bf16[64,768]{1,0:T(8,128)(2,1)S(1)}, u32[]{:S(2)}, u32[]{:S(2)}) collective-permute-start(bf16[64,768]{1,0:T(8,128)(2,1)S(1)} %get-tuple-element.15), channel_id=1, source_target_pairs={{0,64},{64,128},{128,192},{192,0},{1,65},{65,129},{129,193},{193,1... | collective-permute-start | bytes 294920 | tf_op jit(solution)/shard_map/ppermute | solution.py:72
  62.8 10.6 %collective-permute-start.24 = (bf16[64,768]{1,0:T(8,128)(2,1)S(1)}, bf16[64,768]{1,0:T(8,128)(2,1)S(1)}, u32[]{:S(2)}, u32[]{:S(2)}) collective-permute-start(bf16[64,768]{1,0:T(8,128)(2,1)S(1)} %get-tuple-element.16), channel_id=1, source_target_pairs={{0,192},{64,0},{128,64},{192,128},{1,193},{65,1},{129,65},{193,129... | collective-permute-start | bytes 294920 | tf_op jit(solution)/shard_map/ppermute | solution.py:72
  66.5 10.5 %collective-permute-start.23 = (bf16[64,768]{1,0:T(8,128)(2,1)S(1)}, bf16[64,768]{1,0:T(8,128)(2,1)S(1)}, u32[]{:S(2)}, u32[]{:S(2)}) collective-permute-start(bf16[64,768]{1,0:T(8,128)(2,1)S(1)} %get-tuple-element.17), channel_id=1, source_target_pairs={{0,128},{64,192},{128,0},{192,64},{1,129},{65,193},{129,1},{193,65... | collective-permute-start | bytes 294920 | tf_op jit(solution)/shard_map/ppermute | solution.py:72
  77.3 16.3 %collective-permute-start.9 = (bf16[64,768]{1,0:T(8,128)(2,1)S(1)}, bf16[64,768]{1,0:T(8,128)(2,1)S(1)}, u32[]{:S(2)}, u32[]{:S(2)}) collective-permute-start(bf16[64,768]{1,0:T(8,128)(2,1)S(1)} %get-tuple-element.27), channel_id=1, source_target_pairs={{0,128},{64,192},{128,0},{192,64},{1,129},{65,193},{129,1},{193,65... | collective-permute-start | bytes 294920 | tf_op jit(solution)/shard_map/ppermute | solution.py:72
  77.5 8.3 %collective-permute-start.8 = (bf16[64,768]{1,0:T(8,128)(2,1)S(1)}, bf16[64,768]{1,0:T(8,128)(2,1)S(1)}, u32[]{:S(2)}, u32[]{:S(2)}) collective-permute-start(bf16[64,768]{1,0:T(8,128)(2,1)S(1)} %get-tuple-element.27), channel_id=1, source_target_pairs={{0,192},{64,0},{128,64},{192,128},{1,193},{65,1},{129,65},{193,129... | collective-permute-start | bytes 294920 | tf_op jit(solution)/shard_map/ppermute | solution.py:72
  79.7 13.9 %collective-permute-start.10 = (bf16[64,768]{1,0:T(8,128)(2,1)S(1)}, bf16[64,768]{1,0:T(8,128)(2,1)S(1)}, u32[]{:S(2)}, u32[]{:S(2)}) collective-permute-start(bf16[64,768]{1,0:T(8,128)(2,1)S(1)} %get-tuple-element.27), channel_id=1, source_target_pairs={{0,64},{64,128},{128,192},{192,0},{1,65},{65,129},{129,193},{193,1... | collective-permute-start | bytes 294920 | tf_op jit(solution)/shard_map/ppermute | solution.py:72
  80.3 14.8 %collective-permute-start.26 = (bf16[64,768]{1,0:T(8,128)(2,1)S(1)}, bf16[64,768]{1,0:T(8,128)(2,1)S(1)}, u32[]{:S(2)}, u32[]{:S(2)}) collective-permute-start(bf16[64,768]{1,0:T(8,128)(2,1)S(1)} %get-tuple-element.25), channel_id=1, source_target_pairs={{0,128},{64,192},{128,0},{192,64},{1,129},{65,193},{129,1},{193,65... | collective-permute-start | bytes 294920 | tf_op jit(solution)/shard_map/ppermute | solution.py:72
  82.5 12.1 %collective-permute-start.25 = (bf16[64,768]{1,0:T(8,128)(2,1)S(1)}, bf16[64,768]{1,0:T(8,128)(2,1)S(1)}, u32[]{:S(2)}, u32[]{:S(2)}) collective-permute-start(bf16[64,768]{1,0:T(8,128)(2,1)S(1)} %get-tuple-element.25), channel_id=1, source_target_pairs={{0,192},{64,0},{128,64},{192,128},{1,193},{65,1},{129,65},{193,129... | collective-permute-start | bytes 294920 | tf_op jit(solution)/shard_map/ppermute | solution.py:72
  85.7 10.0 %collective-permute-start.27 = (bf16[64,768]{1,0:T(8,128)(2,1)S(1)}, bf16[64,768]{1,0:T(8,128)(2,1)S(1)}, u32[]{:S(2)}, u32[]{:S(2)}) collective-permute-start(bf16[64,768]{1,0:T(8,128)(2,1)S(1)} %get-tuple-element.25), channel_id=1, source_target_pairs={{0,64},{64,128},{128,192},{192,0},{1,65},{65,129},{129,193},{193,1... | collective-permute-start | bytes 294920 | tf_op jit(solution)/shard_map/ppermute | solution.py:72
  101.1 8.1 %collective-permute-start.29 = (bf16[64,3072]{1,0:T(8,128)(2,1)S(1)}, bf16[64,3072]{1,0:T(8,128)(2,1)S(1)}, u32[]{:S(2)}, u32[]{:S(2)}) collective-permute-start(bf16[64,3072]{1,0:T(8,128)(2,1)S(1)} %slice.264), channel_id=1, source_target_pairs={{0,8},{1,3},{2,10},{3,1},{4,12},{5,7},{6,14},{7,5},{8,0},{9,11},{1... | collective-permute-start | bytes 1179656 | tf_op jit(solution)/shard_map/ppermute | solution.py:44
  101.6 9.9 %collective-permute-start.12 = (bf16[64,3072]{1,0:T(8,128)(2,1)S(1)}, bf16[64,3072]{1,0:T(8,128)(2,1)S(1)}, u32[]{:S(2)}, u32[]{:S(2)}) collective-permute-start(bf16[64,3072]{1,0:T(8,128)(2,1)S(1)} %slice.265), channel_id=1, source_target_pairs={{0,24},{1,7},{2,26},{3,5},{4,28},{5,3},{6,30},{7,1},{8,16},{9,15},... | collective-permute-start | bytes 1179656 | tf_op jit(solution)/shard_map/ppermute | solution.py:44
  123.3 10.0 %collective-permute-start.15 = (bf16[8,3072]{1,0:T(8,128)(2,1)S(1)}, bf16[8,3072]{1,0:T(8,128)(2,1)S(1)}, u32[]{:S(2)}, u32[]{:S(2)}) collective-permute-start(bf16[8,3072]{1,0:T(8,128)(2,1)S(1)} %slice.271), channel_id=1, source_target_pairs={{0,2},{1,9},{2,0},{3,11},{4,6},{5,13},{6,4},{7,15},{8,10},{9,1},{1... | collective-permute-start | bytes 147464 | tf_op jit(solution)/shard_map/ppermute | solution.py:44
  125.3 8.1 %collective-permute-start.33 = (bf16[8,3072]{1,0:T(8,128)(2,1)S(1)}, bf16[8,3072]{1,0:T(8,128)(2,1)S(1)}, u32[]{:S(2)}, u32[]{:S(2)}) collective-permute-start(bf16[8,3072]{1,0:T(8,128)(2,1)S(1)} %fusion.34), channel_id=1, source_target_pairs={{0,32},{1,33},{2,34},{3,35},{4,36},{5,37},{6,38},{7,39},{8,40},{9,... | collective-permute-start | bytes 147464 | tf_op jit(solution)/shard_map/ppermute | solution.py:44
  (12 other events, 112.7 us)

commit v2 on v0

v2 whole, which is shorter than its diff:
```python
import math

import jax
import jax.numpy as jnp
from jax import lax
from jax.experimental import pallas as pl
from jax.experimental.pallas import tpu as pltpu
from jax.sharding import PartitionSpec as P

gelu_scale = math.sqrt(2.0 / math.pi)
bf16, f32 = jnp.bfloat16, jnp.float32


def gelu_parts(pre):
    cubic = 0.044715 * pre * pre * pre
    tangent = jnp.tanh(gelu_scale * (pre + cubic))
    gelu_value = 0.5 * pre * (1.0 + tangent)
    gelu_slope = 0.5 * (1.0 + tangent) + 0.5 * pre * (1.0 - tangent * tangent) * gelu_scale * (
        1.0 + 3.0 * 0.044715 * pre * pre
    )
    return (gelu_value, gelu_slope)


def contract(left, right, left_dim, right_dim):
    return lax.dot_general(
        left, right, (((left_dim,), (right_dim,)), ((), ())), preferred_element_type=f32
    )


def move(value, target):
    pairs = []
    for z in range(2):
        for y in range(4):
            for x in range(4):
                for core in range(2):
                    tz, ty, tx, tc = target(z, y, x, core)
                    pairs.append(((z * 4 + y) * 8 + x * 2 + core, (tz * 4 + ty) * 8 + tx * 2 + tc))
    return lax.ppermute(value, ("wt", "out"), pairs)


def swap_z(value):
    return move(value, lambda z, y, x, core: (1 - z, y, x, core))


def swap_core(value):
    return move(value, lambda z, y, x, core: (z, y, x, 1 - core))


def move_chip(value, stage, step):
    def target(z, y, x, core):
        along_x = stage != core
        return (z, y, (x + step) % 4, core) if along_x else (z, (y + step) % 4, x, core)

    return move(value, target)


def gather4(value, stage):
    return [value] + [move_chip(value, stage, -step) for step in (2, 1, 3)]


def sum4(total, stage):
    rows = total.shape[0] // 4
    out = total[:rows].astype(f32)
    for place, step in enumerate((2, 1, 3)):
        block = total[(place + 1) * rows : (place + 2) * rows]
        out = out + move_chip(block.astype(bf16), stage, step).astype(f32)
    return out


def move_inp(value, step):
    return lax.ppermute(value, "inp", [(i, (i + step) % 4) for i in range(4)])


def gather_inp(value):
    return [value] + [move_inp(value, -step) for step in (2, 1, 3)]


def call(kernel, out_shapes, operands, later=(), scratch=()):
    whole = pl.BlockSpec(memory_space=pltpu.VMEM)

    def body(*refs):
        kernel(*refs[: len(operands)], *refs[len(operands) + len(later) :])

    return pl.pallas_call(
        body,
        out_shape=[jax.ShapeDtypeStruct(shape, bf16) for shape in out_shapes],
        in_specs=[whole] * len(operands) + [pl.BlockSpec(memory_space=pl.ANY)] * len(later),
        out_specs=[whole] * len(out_shapes),
        scratch_shapes=list(scratch),
        cost_estimate=pl.CostEstimate(flops=0, bytes_accessed=0, transcendentals=0),
        compiler_params=pltpu.CompilerParams(vmem_limit_bytes=16 * 2**20),
    )(*operands, *later)


def pair_kernel(token, cotangent, out):
    out[:, :3072] = token[...]
    out[:, 3072:] = cotangent[...]


def rows16_kernel(own, other, out):
    out[...] = jnp.concatenate([own[...].astype(f32), other[...].astype(f32)], 0).astype(bf16)


def stack_kernel(*refs):
    rows = refs[0].shape[0]
    for place, piece in enumerate(refs[:-1]):
        refs[-1][pl.ds(place * rows, rows), :] = piece[...]


def stack(pieces, later=()):
    rows, columns = pieces[0].shape
    return call(stack_kernel, [(4 * rows, columns)], pieces, later)[0]


def partials(rows, weight_in, weight_out):
    pre = jnp.dot(rows[:, :3072], weight_in[...], preferred_element_type=f32).astype(bf16)
    return pre, contract(rows[:, 3072:], weight_out[...], 1, 1).astype(bf16)


def own_kernel(rows, weight_in, weight_out, out):
    out[:, :384], out[:, 384:] = partials(rows, weight_in, weight_out)


def other_kernel(rows, weight_in, weight_out, own, *outs):
    outs, full = outs[:4], outs[4]
    full[:256, :] = own[...]
    full[256:, :384], full[256:, 384:] = partials(rows, weight_in, weight_out)
    me = lax.axis_index("inp")
    for step, out in zip((0, 2, 1, 3), outs):
        out[...] = full[pl.ds(pl.multiple_of(lax.rem(me + step, 4) * 128, 128), 128), :]


def gelu_kernel(own, first, second, third, act, grad_pre):
    total = own[...].astype(f32) + first[...].astype(f32) + second[...].astype(f32) + third[...].astype(f32)
    gelu_value, gelu_slope = gelu_parts(total[:, :384])
    act[...] = gelu_value.astype(bf16)
    grad_pre[...] = (total[:, 384:] * gelu_slope).astype(bf16)


def place_kernel(*refs):
    me = lax.axis_index("inp")
    for step, block in zip((0, 2, 1, 3), refs[:4]):
        refs[4][pl.ds(pl.multiple_of(lax.rem(me + step, 4) * 128, 128), 128), :] = block[...]


def place(blocks, later=()):
    return call(place_kernel, [(512, 384)], blocks, later)[0]


def copy_kernel(value, out):
    out[...] = value[...]


def after(value, *later):
    return call(copy_kernel, [value.shape], (value,), later)[0]


def shards(tokens, weight_in, weight_out, cotangent):
    rows = call(pair_kernel, [(8, 6144)], (tokens, cotangent))[0]
    rows = call(rows16_kernel, [(16, 6144)], (rows, swap_z(rows)))[0]
    rows = stack(gather4(rows, 0))
    own = stack(gather4(rows, 1))
    other = swap_core(own)
    weights = (weight_in, weight_out)
    partial = call(own_kernel, [(256, 768)], (own, *weights))[0]
    blocks = call(other_kernel, [(128, 768)] * 4, (other, *weights, partial), scratch=[pltpu.VMEM((512, 768), bf16)])
    moved = [move_inp(block, step) for step, block in zip((2, 1, 3), blocks[1:])]
    act, grad_pre = call(gelu_kernel, [(128, 384)] * 2, (blocks[0], *moved))
    grad_pre = place(gather_inp(grad_pre))
    sent = contract(grad_pre[256:], weight_in, 1, 1).astype(bf16)
    act = gather_inp(after(act, sent))
    total = contract(grad_pre[:256], weight_in, 1, 1) + swap_core(sent).astype(f32)
    grad_weight_in = contract(own[:, :3072], grad_pre[:256], 0, 0) + contract(other[:, :3072], grad_pre[256:], 0, 0)
    total = sum4(total, 1)
    total = sum4(total, 0)
    last = total[8:].astype(bf16)
    grad_tokens = total[:8] + swap_z(last).astype(f32)
    act = place(act)
    grad_weight_out = contract(act[:256], own[:, 3072:], 0, 0) + contract(act[256:], other[:, 3072:], 0, 0)
    return (grad_tokens.astype(bf16), grad_weight_in.astype(bf16), grad_weight_out.astype(bf16))


def solution(mesh):
    in_specs = (
        P(("wt", "out"), "inp"),
        P("inp", ("wt", "out")),
        P(("wt", "out"), "inp"),
        P(("wt", "out"), "inp"),
    )
    out_specs = (P(("wt", "out"), "inp"), P("inp", ("wt", "out")), P(("wt", "out"), "inp"))
    return jax.shard_map(shards, mesh=mesh, in_specs=in_specs, out_specs=out_specs, check_vma=False)
```

time: 451 us -> 125 us (0.28)
  waiting for transfers between devices: 377 us -> 59.6 us
  starting transfers between devices: 0.2 us -> 49.2 us
  blocking collectives: 29.3 us -> 0 us
  matrix products: 23.7 us -> 8.58 us
  between operations: 13.8 us -> 0.82 us
    reduce_scatter x3 -> x0, waiting for transfers between devices: 202 us -> none  [the longest x1 153 us: shards(): lax.psum_scatter(contract(row_block, weight_in, 1, 1), ('wt', 'out'), sca...]
    all_gather x2 -> x0, waiting for transfers between devices: 173 us -> none  [the longest x1 92.4 us: shards(): token_full = lax.all_gather(tokens, ('wt', 'out'), axis=0, tiled=True)]
    ppermute x0 -> x25, waiting for transfers between devices: none -> 59.6 us  [the longest x16 41.8 us: move(): return lax.ppermute(value, ('wt', 'out'), pairs)]
    ppermute x0 -> x25, starting transfers between devices: none -> 49.2 us  [the longest x16 30.9 us: move(): return lax.ppermute(value, ('wt', 'out'), pairs)]
    all_gather x2 -> x0, blocking collectives: 29.3 us -> none  [the longest x1 15 us: shards(): grad_pre_full = lax.all_gather(grad_pre_local, 'inp', axis=0, tiled=True)]
    dot_general x4 -> x6, matrix products: 19.3 us -> 8.58 us  [contract(): lax.dot_general(left, right, (((left_dim,), (right_dim,)), ((), ())), pre...]
  transfers between devices with their start and end apart: 5 -> 25, of which waited for: 5 -> 20; matrix products, arithmetic and copies ran while one was open for 5% -> 6% of each run, Pallas kernels for 0% -> 1%
where the time goes in v2:
time: 125 us
  waiting for transfers between devices  59.6 us (48%)
  starting transfers between devices  49.2 us (39%)
  matrix products  8.58 us (7%)
  Pallas kernels  4.28 us (3%)
  local copies, waits for them, and re-layouts  1.71 us (1%)
    ppermute x16, waiting for transfers between devices, move(): return lax.ppermute(value, ('wt', 'out'), pairs)  41.8 us
    ppermute x16, starting transfers between devices, move(): return lax.ppermute(value, ('wt', 'out'), pairs)  30.9 us
    ppermute x9, starting transfers between devices, move_inp(): return lax.ppermute(value, 'inp', [(i, (i + step) % 4) for i in range(4)])  18.3 us
    ppermute x9, waiting for transfers between devices, move_inp(): return lax.ppermute(value, 'inp', [(i, (i + step) % 4) for i in range(4)])  17.8 us
    dot_general x6, matrix products, contract(): lax.dot_general(left, right, (((left_dim,), (right_dim,)), ((), ())), pre...  8.58 us
    pallas_call x10, Pallas kernels, call(): pl.pallas_call(body, out_shape=[jax.ShapeDtypeStruct(shape, bf16) for sha...  4.28 us
  transfers between devices with their start and end apart: 25, of which 20 were waited for; matrix products, arithmetic and copies ran while one was open for 6% of the time, Pallas kernels for 1%

profile of v2, /device:TPU:2, one launch (start us, length us, event | category | flops | bytes accessed | tf_op | source)
XLA Modules:
  0.0 125.1 jit_solution(16818747781549076982)
XLA Ops:
  2.2 7.3 %collective-permute-start = (bf16[8,6144]{1,0:T(8,128)(2,1)S(1)}, bf16[8,6144]{1,0:T(8,128)(2,1)S(1)}, u32[]{:S(2)}, u32[]{:S(2)}) collective-permute-start(bf16[8,6144]{1,0:T(8,128)(2,1)S(1)} %shard_map.67.refs_0_), channel_id=1, source_target_pairs={{0,32},{1,33},{2,34},{3,35},{4,36},{5,37},{6,38},{7,39},{8,40},{9,... | collective-permute-start | bytes 294920 | tf_op jit(solution)/shard_map/ppermute | solution.py:38
  9.5 2.9 %collective-permute-done.refs_1_ = bf16[8,6144]{1,0:T(8,128)(2,1)S(1)} collective-permute-done((bf16[8,6144]{1,0:T(8,128)(2,1)S(1)}, bf16[8,6144]{1,0:T(8,128)(2,1)S(1)}, u32[]{:S(2)}, u32[]{:S(2)}) %collective-permute-start) | collective-permute-done | bytes 98336 | tf_op jit(solution)/shard_map/ppermute | solution.py:38
  15.7 2.0 %collective-permute-start.1 = (bf16[16,6144]{1,0:T(8,128)(2,1)S(1)}, bf16[16,6144]{1,0:T(8,128)(2,1)S(1)}, u32[]{:S(2)}, u32[]{:S(2)}) collective-permute-start(bf16[16,6144]{1,0:T(8,128)(2,1)S(1)} %shard_map.68.refs_0_), channel_id=1, source_target_pairs={{0,16},{1,5},{2,18},{3,7},{4,20},{5,1},{6,22},{7,3},{8,24},{9,13},... | collective-permute-start | bytes 589832 | tf_op jit(solution)/shard_map/ppermute | solution.py:38
  19.7 3.2 %collective-permute-done.1.refs_1_ = bf16[16,6144]{1,0:T(8,128)(2,1)S(1)} collective-permute-done((bf16[16,6144]{1,0:T(8,128)(2,1)S(1)}, bf16[16,6144]{1,0:T(8,128)(2,1)S(1)}, u32[]{:S(2)}, u32[]{:S(2)}) %collective-permute-start.1) | collective-permute-done | bytes 196640 | tf_op jit(solution)/shard_map/ppermute | solution.py:38
  25.1 2.1 %collective-permute-start.4 = (bf16[64,6144]{1,0:T(8,128)(2,1)S(1)}, bf16[64,6144]{1,0:T(8,128)(2,1)S(1)}, u32[]{:S(2)}, u32[]{:S(2)}) collective-permute-start(bf16[64,6144]{1,0:T(8,128)(2,1)S(1)} %shard_map.69.refs_0_), channel_id=1, source_target_pairs={{0,4},{1,17},{2,6},{3,19},{4,0},{5,21},{6,2},{7,23},{8,12},{9,25},... | collective-permute-start | bytes 2359304 | tf_op jit(solution)/shard_map/ppermute | solution.py:38
  27.2 7.8 %collective-permute-done.6.refs_3_ = bf16[64,6144]{1,0:T(8,128)(2,1)S(1)} collective-permute-done((bf16[64,6144]{1,0:T(8,128)(2,1)S(1)}, bf16[64,6144]{1,0:T(8,128)(2,1)S(1)}, u32[]{:S(2)}, u32[]{:S(2)}) %collective-permute-start.6) | collective-permute-done | bytes 786464 | tf_op jit(solution)/shard_map/ppermute | solution.py:38
  36.6 9.1 %collective-permute-done.4.refs_1_ = bf16[64,6144]{1,0:T(8,128)(2,1)S(1)} collective-permute-done((bf16[64,6144]{1,0:T(8,128)(2,1)S(1)}, bf16[64,6144]{1,0:T(8,128)(2,1)S(1)}, u32[]{:S(2)}, u32[]{:S(2)}) %collective-permute-start.4) | collective-permute-done | bytes 786464 | tf_op jit(solution)/shard_map/ppermute | solution.py:38
  47.7 3.8 %collective-permute-done.7.refs_0_ = bf16[256,6144]{1,0:T(8,128)(2,1)S(1)} collective-permute-done((bf16[256,6144]{1,0:T(8,128)(2,1)S(1)}, bf16[256,6144]{1,0:T(8,128)(2,1)S(1)}, u32[]{:S(2)}, u32[]{:S(2)}) %collective-permute-start.7) | collective-permute-done | bytes 3145760 | tf_op jit(solution)/shard_map/ppermute | solution.py:38
  53.4 3.9 %collective-permute-start.8 = (bf16[128,768]{1,0:T(8,128)(2,1)S(1)}, bf16[128,768]{1,0:T(8,128)(2,1)S(1)}, u32[]{:S(2)}, u32[]{:S(2)}) collective-permute-start(bf16[128,768]{1,0:T(8,128)(2,1)S(1)} %get-tuple-element.10), channel_id=1, source_target_pairs={{0,128},{64,192},{128,0},{192,64},{1,129},{65,193},{129,1},{193,65... | collective-permute-start | bytes 589832 | tf_op jit(solution)/shard_map/ppermute | solution.py:71
  57.4 3.8 %collective-permute-start.10 = (bf16[128,768]{1,0:T(8,128)(2,1)S(1)}, bf16[128,768]{1,0:T(8,128)(2,1)S(1)}, u32[]{:S(2)}, u32[]{:S(2)}) collective-permute-start(bf16[128,768]{1,0:T(8,128)(2,1)S(1)} %get-tuple-element.12), channel_id=1, source_target_pairs={{0,192},{64,0},{128,64},{192,128},{1,193},{65,1},{129,65},{193,129... | collective-permute-start | bytes 589832 | tf_op jit(solution)/shard_map/ppermute | solution.py:71
  61.2 10.3 %collective-permute-done.8.refs_1_ = bf16[128,768]{1,0:T(8,128)(2,1)S(1)} collective-permute-done((bf16[128,768]{1,0:T(8,128)(2,1)S(1)}, bf16[128,768]{1,0:T(8,128)(2,1)S(1)}, u32[]{:S(2)}, u32[]{:S(2)}) %collective-permute-start.8) | collective-permute-done | bytes 196640 | tf_op jit(solution)/shard_map/ppermute | solution.py:71
  72.0 4.2 %collective-permute-start.13 = (bf16[128,384]{1,0:T(8,128)(2,1)S(1)}, bf16[128,384]{1,0:T(8,128)(2,1)S(1)}, u32[]{:S(2)}, u32[]{:S(2)}) collective-permute-start(bf16[128,384]{1,0:T(8,128)(2,1)S(1)} %get-tuple-element.13.refs_0_), channel_id=1, source_target_pairs={{0,64},{64,128},{128,192},{192,0},{1,65},{65,129},{129,193},{193,1... | collective-permute-start | bytes 294920 | tf_op jit(solution)/shard_map/ppermute | solution.py:71
  76.2 2.4 %collective-permute-start.11 = (bf16[128,384]{1,0:T(8,128)(2,1)S(1)}, bf16[128,384]{1,0:T(8,128)(2,1)S(1)}, u32[]{:S(2)}, u32[]{:S(2)}) collective-permute-start(bf16[128,384]{1,0:T(8,128)(2,1)S(1)} %get-tuple-element.13.refs_0_), channel_id=1, source_target_pairs={{0,128},{64,192},{128,0},{192,64},{1,129},{65,193},{129,1},{193,65... | collective-permute-start | bytes 294920 | tf_op jit(solution)/shard_map/ppermute | solution.py:71
  79.4 2.1 %collective-permute-done.12.refs_2_ = bf16[128,384]{1,0:T(8,128)(2,1)S(1)} collective-permute-done((bf16[128,384]{1,0:T(8,128)(2,1)S(1)}, bf16[128,384]{1,0:T(8,128)(2,1)S(1)}, u32[]{:S(2)}, u32[]{:S(2)}) %collective-permute-start.12) | collective-permute-done | bytes 98336 | tf_op jit(solution)/shard_map/ppermute | solution.py:71
  81.5 3.3 %collective-permute-done.11.refs_1_ = bf16[128,384]{1,0:T(8,128)(2,1)S(1)} collective-permute-done((bf16[128,384]{1,0:T(8,128)(2,1)S(1)}, bf16[128,384]{1,0:T(8,128)(2,1)S(1)}, u32[]{:S(2)}, u32[]{:S(2)}) %collective-permute-start.11) | collective-permute-done | bytes 98336 | tf_op jit(solution)/shard_map/ppermute | solution.py:71
  86.6 3.3 %collective-permute-start.23 = (bf16[128,384]{1,0:T(8,128)(2,1)S(1)}, bf16[128,384]{1,0:T(8,128)(2,1)S(1)}, u32[]{:S(2)}, u32[]{:S(2)}) collective-permute-start(bf16[128,384]{1,0:T(8,128)(2,1)S(1)} %shard_map.75.refs_0_), channel_id=1, source_target_pairs={{0,192},{64,0},{128,64},{192,128},{1,193},{65,1},{129,65},{193,129... | collective-permute-start | bytes 294920 | tf_op jit(solution)/shard_map/ppermute | solution.py:71
  94.0 2.0 %collective-permute-start.16 = (bf16[64,3072]{1,0:T(8,128)(2,1)S(1)}, bf16[64,3072]{1,0:T(8,128)(2,1)S(1)}, u32[]{:S(2)}, u32[]{:S(2)}) collective-permute-start(bf16[64,3072]{1,0:T(8,128)(2,1)S(1)} %get-tuple-element.19), channel_id=1, source_target_pairs={{0,2},{1,9},{2,4},{3,11},{4,6},{5,13},{6,0},{7,15},{8,10},{9,17},{... | collective-permute-start | bytes 1179656 | tf_op jit(solution)/shard_map/ppermute | solution.py:38
  96.0 2.4 %add_convert_fusion.1 = bf16[3072,384]{1,0:T(8,128)(2,1)} fusion(f32[3072,384]{1,0:T(8,128)S(1)} %fusion.3, bf16[256,6144]{1,0:T(8,128)(2,1)S(1)} %shard_map.70.refs_0_, bf16[512,384]{1,0:T(8,128)(2,1)S(1)} %shard_map.74), kind=kOutput, calls=%fused_computation.1 | convolution fusion | flops 606339072 | bytes 8847360 | tf_op jit(solution)/shard_map/dot_general | solution.py:25
  99.5 2.2 %collective-permute-done.15 = bf16[64,3072]{1,0:T(8,128)(2,1)S(1)} collective-permute-done((bf16[64,3072]{1,0:T(8,128)(2,1)S(1)}, bf16[64,3072]{1,0:T(8,128)(2,1)S(1)}, u32[]{:S(2)}, u32[]{:S(2)}) %collective-permute-start.15) | collective-permute-done | bytes 393248 | tf_op jit(solution)/shard_map/ppermute | solution.py:38
  101.6 4.1 %collective-permute-done.17 = bf16[64,3072]{1,0:T(8,128)(2,1)S(1)} collective-permute-done((bf16[64,3072]{1,0:T(8,128)(2,1)S(1)}, bf16[64,3072]{1,0:T(8,128)(2,1)S(1)}, u32[]{:S(2)}, u32[]{:S(2)}) %collective-permute-start.17) | collective-permute-done | bytes 393248 | tf_op jit(solution)/shard_map/ppermute | solution.py:38
  106.0 2.1 %collective-permute-start.18 = (bf16[16,3072]{1,0:T(8,128)(2,1)S(1)}, bf16[16,3072]{1,0:T(8,128)(2,1)S(1)}, u32[]{:S(2)}, u32[]{:S(2)}) collective-permute-start(bf16[16,3072]{1,0:T(8,128)(2,1)S(1)} %get-tuple-element.20), channel_id=1, source_target_pairs={{0,16},{1,5},{2,18},{3,7},{4,20},{5,1},{6,22},{7,3},{8,24},{9,13},... | collective-permute-start | bytes 294920 | tf_op jit(solution)/shard_map/ppermute | solution.py:38
  112.7 3.1 %collective-permute-done.19 = bf16[16,3072]{1,0:T(8,128)(2,1)S(1)} collective-permute-done((bf16[16,3072]{1,0:T(8,128)(2,1)S(1)}, bf16[16,3072]{1,0:T(8,128)(2,1)S(1)}, u32[]{:S(2)}, u32[]{:S(2)}) %collective-permute-start.19) | collective-permute-done | bytes 98336 | tf_op jit(solution)/shard_map/ppermute | solution.py:38
  115.9 6.0 %collective-permute-start.21 = (bf16[8,3072]{1,0:T(8,128)(2,1)S(1)}, bf16[8,3072]{1,0:T(8,128)(2,1)S(1)}, u32[]{:S(2)}, u32[]{:S(2)}) collective-permute-start(bf16[8,3072]{1,0:T(8,128)(2,1)S(1)} %slice.133), channel_id=1, source_target_pairs={{0,32},{1,33},{2,34},{3,35},{4,36},{5,37},{6,38},{7,39},{8,40},{9,... | collective-permute-start | bytes 147464 | tf_op jit(solution)/shard_map/ppermute | solution.py:38
  121.9 2.2 %add_convert_fusion = bf16[384,3072]{1,0:T(8,128)(2,1)} fusion(f32[384,3072]{1,0:T(8,128)S(1)} %fusion, bf16[256,6144]{1,0:T(8,128)(2,1)S(1)} %shard_map.70.refs_0_, bf16[512,384]{1,0:T(8,128)(2,1)S(1)} %shard_map.76), kind=kOutput, calls=%fused_computation | convolution fusion | flops 606339072 | bytes 8847360 | tf_op jit(solution)/shard_map/dot_general | solution.py:25
  (56 shorter events, 28.5 us)
Async XLA Ops:
  2.2 10.2 %collective-permute-start = (bf16[8,6144]{1,0:T(8,128)(2,1)S(1)}, bf16[8,6144]{1,0:T(8,128)(2,1)S(1)}, u32[]{:S(2)}, u32[]{:S(2)}) collective-permute-start(bf16[8,6144]{1,0:T(8,128)(2,1)S(1)} %shard_map.67.refs_0_), channel_id=1, source_target_pairs={{0,32},{1,33},{2,34},{3,35},{4,36},{5,37},{6,38},{7,39},{8,40},{9,... | collective-permute-start | bytes 294920 | tf_op jit(solution)/shard_map/ppermute | solution.py:38
  12.4 7.0 %collective-permute-start.3 = (bf16[16,6144]{1,0:T(8,128)(2,1)S(1)}, bf16[16,6144]{1,0:T(8,128)(2,1)S(1)}, u32[]{:S(2)}, u32[]{:S(2)}) collective-permute-start(bf16[16,6144]{1,0:T(8,128)(2,1)S(1)} %shard_map.68.refs_0_), channel_id=1, source_target_pairs={{0,8},{1,3},{2,10},{3,5},{4,12},{5,7},{6,14},{7,1},{8,16},{9,11},{... | collective-permute-start | bytes 589832 | tf_op jit(solution)/shard_map/ppermute | solution.py:38
  14.1 5.7 %collective-permute-start.2 = (bf16[16,6144]{1,0:T(8,128)(2,1)S(1)}, bf16[16,6144]{1,0:T(8,128)(2,1)S(1)}, u32[]{:S(2)}, u32[]{:S(2)}) collective-permute-start(bf16[16,6144]{1,0:T(8,128)(2,1)S(1)} %shard_map.68.refs_0_), channel_id=1, source_target_pairs={{0,24},{1,7},{2,26},{3,1},{4,28},{5,3},{6,30},{7,5},{8,0},{9,15},{... | collective-permute-start | bytes 589832 | tf_op jit(solution)/shard_map/ppermute | solution.py:38
  15.7 7.2 %collective-permute-start.1 = (bf16[16,6144]{1,0:T(8,128)(2,1)S(1)}, bf16[16,6144]{1,0:T(8,128)(2,1)S(1)}, u32[]{:S(2)}, u32[]{:S(2)}) collective-permute-start(bf16[16,6144]{1,0:T(8,128)(2,1)S(1)} %shard_map.68.refs_0_), channel_id=1, source_target_pairs={{0,16},{1,5},{2,18},{3,7},{4,20},{5,1},{6,22},{7,3},{8,24},{9,13},... | collective-permute-start | bytes 589832 | tf_op jit(solution)/shard_map/ppermute | solution.py:38
  23.0 12.1 %collective-permute-start.6 = (bf16[64,6144]{1,0:T(8,128)(2,1)S(1)}, bf16[64,6144]{1,0:T(8,128)(2,1)S(1)}, u32[]{:S(2)}, u32[]{:S(2)}) collective-permute-start(bf16[64,6144]{1,0:T(8,128)(2,1)S(1)} %shard_map.69.refs_0_), channel_id=1, source_target_pairs={{0,2},{1,9},{2,4},{3,11},{4,6},{5,13},{6,0},{7,15},{8,10},{9,17},{... | collective-permute-start | bytes 2359304 | tf_op jit(solution)/shard_map/ppermute | solution.py:38
  24.6 12.0 %collective-permute-start.5 = (bf16[64,6144]{1,0:T(8,128)(2,1)S(1)}, bf16[64,6144]{1,0:T(8,128)(2,1)S(1)}, u32[]{:S(2)}, u32[]{:S(2)}) collective-permute-start(bf16[64,6144]{1,0:T(8,128)(2,1)S(1)} %shard_map.69.refs_0_), channel_id=1, source_target_pairs={{0,6},{1,25},{2,0},{3,27},{4,2},{5,29},{6,4},{7,31},{8,14},{9,1},{... | collective-permute-start | bytes 2359304 | tf_op jit(solution)/shard_map/ppermute | solution.py:38
  25.1 20.5 %collective-permute-start.4 = (bf16[64,6144]{1,0:T(8,128)(2,1)S(1)}, bf16[64,6144]{1,0:T(8,128)(2,1)S(1)}, u32[]{:S(2)}, u32[]{:S(2)}) collective-permute-start(bf16[64,6144]{1,0:T(8,128)(2,1)S(1)} %shard_map.69.refs_0_), channel_id=1, source_target_pairs={{0,4},{1,17},{2,6},{3,19},{4,0},{5,21},{6,2},{7,23},{8,12},{9,25},... | collective-permute-start | bytes 2359304 | tf_op jit(solution)/shard_map/ppermute | solution.py:38
  45.8 5.7 %collective-permute-start.7 = (bf16[256,6144]{1,0:T(8,128)(2,1)S(1)}, bf16[256,6144]{1,0:T(8,128)(2,1)S(1)}, u32[]{:S(2)}, u32[]{:S(2)}) collective-permute-start(bf16[256,6144]{1,0:T(8,128)(2,1)S(1)} %shard_map.70.refs_0_), channel_id=1, source_target_pairs={{0,1},{1,0},{2,3},{3,2},{4,5},{5,4},{6,7},{7,6},{8,9},{9,8},{10,11... | collective-permute-start | bytes 9437192 | tf_op jit(solution)/shard_map/ppermute | solution.py:38
  53.4 18.1 %collective-permute-start.8 = (bf16[128,768]{1,0:T(8,128)(2,1)S(1)}, bf16[128,768]{1,0:T(8,128)(2,1)S(1)}, u32[]{:S(2)}, u32[]{:S(2)}) collective-permute-start(bf16[128,768]{1,0:T(8,128)(2,1)S(1)} %get-tuple-element.10), channel_id=1, source_target_pairs={{0,128},{64,192},{128,0},{192,64},{1,129},{65,193},{129,1},{193,65... | collective-permute-start | bytes 589832 | tf_op jit(solution)/shard_map/ppermute | solution.py:71
  57.4 14.2 %collective-permute-start.9 = (bf16[128,768]{1,0:T(8,128)(2,1)S(1)}, bf16[128,768]{1,0:T(8,128)(2,1)S(1)}, u32[]{:S(2)}, u32[]{:S(2)}) collective-permute-start(bf16[128,768]{1,0:T(8,128)(2,1)S(1)} %get-tuple-element.11), channel_id=1, source_target_pairs={{0,64},{64,128},{128,192},{192,0},{1,65},{65,129},{129,193},{193,1... | collective-permute-start | bytes 589832 | tf_op jit(solution)/shard_map/ppermute | solution.py:71
  57.4 14.4 %collective-permute-start.10 = (bf16[128,768]{1,0:T(8,128)(2,1)S(1)}, bf16[128,768]{1,0:T(8,128)(2,1)S(1)}, u32[]{:S(2)}, u32[]{:S(2)}) collective-permute-start(bf16[128,768]{1,0:T(8,128)(2,1)S(1)} %get-tuple-element.12), channel_id=1, source_target_pairs={{0,192},{64,0},{128,64},{192,128},{1,193},{65,1},{129,65},{193,129... | collective-permute-start | bytes 589832 | tf_op jit(solution)/shard_map/ppermute | solution.py:71
  72.0 7.4 %collective-permute-start.13 = (bf16[128,384]{1,0:T(8,128)(2,1)S(1)}, bf16[128,384]{1,0:T(8,128)(2,1)S(1)}, u32[]{:S(2)}, u32[]{:S(2)}) collective-permute-start(bf16[128,384]{1,0:T(8,128)(2,1)S(1)} %get-tuple-element.13.refs_0_), channel_id=1, source_target_pairs={{0,64},{64,128},{128,192},{192,0},{1,65},{65,129},{129,193},{193,1... | collective-permute-start | bytes 294920 | tf_op jit(solution)/shard_map/ppermute | solution.py:71
  76.1 5.4 %collective-permute-start.12 = (bf16[128,384]{1,0:T(8,128)(2,1)S(1)}, bf16[128,384]{1,0:T(8,128)(2,1)S(1)}, u32[]{:S(2)}, u32[]{:S(2)}) collective-permute-start(bf16[128,384]{1,0:T(8,128)(2,1)S(1)} %get-tuple-element.13.refs_0_), channel_id=1, source_target_pairs={{0,192},{64,0},{128,64},{192,128},{1,193},{65,1},{129,65},{193,129... | collective-permute-start | bytes 294920 | tf_op jit(solution)/shard_map/ppermute | solution.py:71
  76.2 8.6 %collective-permute-start.11 = (bf16[128,384]{1,0:T(8,128)(2,1)S(1)}, bf16[128,384]{1,0:T(8,128)(2,1)S(1)}, u32[]{:S(2)}, u32[]{:S(2)}) collective-permute-start(bf16[128,384]{1,0:T(8,128)(2,1)S(1)} %get-tuple-element.13.refs_0_), channel_id=1, source_target_pairs={{0,128},{64,192},{128,0},{192,64},{1,129},{65,193},{129,1},{193,65... | collective-permute-start | bytes 294920 | tf_op jit(solution)/shard_map/ppermute | solution.py:71
  85.9 5.1 %collective-permute-start.14 = (bf16[256,3072]{1,0:T(8,128)(2,1)S(1)}, bf16[256,3072]{1,0:T(8,128)(2,1)S(1)}, u32[]{:S(2)}, u32[]{:S(2)}) collective-permute-start(bf16[256,3072]{1,0:T(8,128)(2,1)S(1)} %convolution_convert_fusion.refs_1_), channel_id=1, source_target_pairs={{0,1},{1,0},{2,3},{3,2},{4,5},{5,4},{6,7},{7,6},{8,9},{9,8},{10,11... | collective-permute-start | bytes 4718600 | tf_op jit(solution)/shard_map/ppermute | solution.py:38
  86.0 7.9 %collective-permute-start.24 = (bf16[128,384]{1,0:T(8,128)(2,1)S(1)}, bf16[128,384]{1,0:T(8,128)(2,1)S(1)}, u32[]{:S(2)}, u32[]{:S(2)}) collective-permute-start(bf16[128,384]{1,0:T(8,128)(2,1)S(1)} %shard_map.75.refs_0_), channel_id=1, source_target_pairs={{0,64},{64,128},{128,192},{192,0},{1,65},{65,129},{129,193},{193,1... | collective-permute-start | bytes 294920 | tf_op jit(solution)/shard_map/ppermute | solution.py:71
  86.6 11.8 %collective-permute-start.23 = (bf16[128,384]{1,0:T(8,128)(2,1)S(1)}, bf16[128,384]{1,0:T(8,128)(2,1)S(1)}, u32[]{:S(2)}, u32[]{:S(2)}) collective-permute-start(bf16[128,384]{1,0:T(8,128)(2,1)S(1)} %shard_map.75.refs_0_), channel_id=1, source_target_pairs={{0,192},{64,0},{128,64},{192,128},{1,193},{65,1},{129,65},{193,129... | collective-permute-start | bytes 294920 | tf_op jit(solution)/shard_map/ppermute | solution.py:71
  89.9 9.5 %collective-permute-start.22 = (bf16[128,384]{1,0:T(8,128)(2,1)S(1)}, bf16[128,384]{1,0:T(8,128)(2,1)S(1)}, u32[]{:S(2)}, u32[]{:S(2)}) collective-permute-start(bf16[128,384]{1,0:T(8,128)(2,1)S(1)} %shard_map.75.refs_0_), channel_id=1, source_target_pairs={{0,128},{64,192},{128,0},{192,64},{1,129},{65,193},{129,1},{193,65... | collective-permute-start | bytes 294920 | tf_op jit(solution)/shard_map/ppermute | solution.py:71
  92.2 9.5 %collective-permute-start.15 = (bf16[64,3072]{1,0:T(8,128)(2,1)S(1)}, bf16[64,3072]{1,0:T(8,128)(2,1)S(1)}, u32[]{:S(2)}, u32[]{:S(2)}) collective-permute-start(bf16[64,3072]{1,0:T(8,128)(2,1)S(1)} %get-tuple-element.17), channel_id=1, source_target_pairs={{0,4},{1,17},{2,6},{3,19},{4,0},{5,21},{6,2},{7,23},{8,12},{9,25},... | collective-permute-start | bytes 1179656 | tf_op jit(solution)/shard_map/ppermute | solution.py:38
  94.0 11.8 %collective-permute-start.17 = (bf16[64,3072]{1,0:T(8,128)(2,1)S(1)}, bf16[64,3072]{1,0:T(8,128)(2,1)S(1)}, u32[]{:S(2)}, u32[]{:S(2)}) collective-permute-start(bf16[64,3072]{1,0:T(8,128)(2,1)S(1)} %get-tuple-element.18), channel_id=1, source_target_pairs={{0,6},{1,25},{2,0},{3,27},{4,2},{5,29},{6,4},{7,31},{8,14},{9,1},{... | collective-permute-start | bytes 1179656 | tf_op jit(solution)/shard_map/ppermute | solution.py:38
  94.0 11.8 %collective-permute-start.16 = (bf16[64,3072]{1,0:T(8,128)(2,1)S(1)}, bf16[64,3072]{1,0:T(8,128)(2,1)S(1)}, u32[]{:S(2)}, u32[]{:S(2)}) collective-permute-start(bf16[64,3072]{1,0:T(8,128)(2,1)S(1)} %get-tuple-element.19), channel_id=1, source_target_pairs={{0,2},{1,9},{2,4},{3,11},{4,6},{5,13},{6,0},{7,15},{8,10},{9,17},{... | collective-permute-start | bytes 1179656 | tf_op jit(solution)/shard_map/ppermute | solution.py:38
  106.0 6.2 %collective-permute-start.18 = (bf16[16,3072]{1,0:T(8,128)(2,1)S(1)}, bf16[16,3072]{1,0:T(8,128)(2,1)S(1)}, u32[]{:S(2)}, u32[]{:S(2)}) collective-permute-start(bf16[16,3072]{1,0:T(8,128)(2,1)S(1)} %get-tuple-element.20), channel_id=1, source_target_pairs={{0,16},{1,5},{2,18},{3,7},{4,20},{5,1},{6,22},{7,3},{8,24},{9,13},... | collective-permute-start | bytes 294920 | tf_op jit(solution)/shard_map/ppermute | solution.py:38
  110.0 5.8 %collective-permute-start.19 = (bf16[16,3072]{1,0:T(8,128)(2,1)S(1)}, bf16[16,3072]{1,0:T(8,128)(2,1)S(1)}, u32[]{:S(2)}, u32[]{:S(2)}) collective-permute-start(bf16[16,3072]{1,0:T(8,128)(2,1)S(1)} %get-tuple-element.22), channel_id=1, source_target_pairs={{0,8},{1,3},{2,10},{3,5},{4,12},{5,7},{6,14},{7,1},{8,16},{9,11},{... | collective-permute-start | bytes 294920 | tf_op jit(solution)/shard_map/ppermute | solution.py:38
  115.9 8.6 %collective-permute-start.21 = (bf16[8,3072]{1,0:T(8,128)(2,1)S(1)}, bf16[8,3072]{1,0:T(8,128)(2,1)S(1)}, u32[]{:S(2)}, u32[]{:S(2)}) collective-permute-start(bf16[8,3072]{1,0:T(8,128)(2,1)S(1)} %slice.133), channel_id=1, source_target_pairs={{0,32},{1,33},{2,34},{3,35},{4,36},{5,37},{6,38},{7,39},{8,40},{9,... | collective-permute-start | bytes 147464 | tf_op jit(solution)/shard_map/ppermute | solution.py:38
  (5 other events, 52.1 us)

commit v3 on v2

v3 whole, which is shorter than its diff:
```python
import math

import jax
import jax.numpy as jnp
from jax import lax
from jax.experimental import pallas as pl
from jax.experimental.pallas import tpu as pltpu
from jax.sharding import PartitionSpec as P

gelu_scale = math.sqrt(2.0 / math.pi)
bf16, f32 = jnp.bfloat16, jnp.float32


def gelu_parts(pre):
    cubic = 0.044715 * pre * pre * pre
    tangent = jnp.tanh(gelu_scale * (pre + cubic))
    gelu_value = 0.5 * pre * (1.0 + tangent)
    gelu_slope = 0.5 * (1.0 + tangent) + 0.5 * pre * (1.0 - tangent * tangent) * gelu_scale * (
        1.0 + 3.0 * 0.044715 * pre * pre
    )
    return (gelu_value, gelu_slope)


def contract(left, right, left_dim, right_dim):
    return lax.dot_general(
        left, right, (((left_dim,), (right_dim,)), ((), ())), preferred_element_type=f32
    )


def move(value, target):
    pairs = []
    for z in range(2):
        for y in range(4):
            for x in range(4):
                for core in range(2):
                    tz, ty, tx, tc = target(z, y, x, core)
                    pairs.append(((z * 4 + y) * 8 + x * 2 + core, (tz * 4 + ty) * 8 + tx * 2 + tc))
    return lax.ppermute(value, ("wt", "out"), pairs)


def swap_z(value):
    return move(value, lambda z, y, x, core: (1 - z, y, x, core))


def swap_core(value):
    return move(value, lambda z, y, x, core: (z, y, x, 1 - core))


def move_chip(value, stage, step):
    def target(z, y, x, core):
        along_x = stage != core
        return (z, y, (x + step) % 4, core) if along_x else (z, (y + step) % 4, x, core)

    return move(value, target)


def gather4(value, stage):
    return [value] + [move_chip(value, stage, -step) for step in (2, 1, 3)]


def scatter(blocks, stage, steps):
    return [move_chip(block, stage, step) for block, step in zip(blocks, steps)]


def move_inp(value, step):
    return lax.ppermute(value, "inp", [(i, (i + step) % 4) for i in range(4)])


def gather_inp(value):
    return [value] + [move_inp(value, -step) for step in (2, 1, 3)]


WHOLE = pl.BlockSpec(memory_space=pltpu.VMEM)


def call(kernel, outs, operands, later=(), scratch=(), in_specs=None, **kwargs):
    def body(*refs):
        kernel(*refs[: len(operands)], *refs[len(operands) + len(later) :])

    in_specs = in_specs or [WHOLE] * len(operands)
    return pl.pallas_call(
        body,
        out_shape=[out if isinstance(out, jax.ShapeDtypeStruct) else jax.ShapeDtypeStruct(out, bf16) for out in outs],
        in_specs=in_specs + [pl.BlockSpec(memory_space=pl.ANY)] * len(later),
        out_specs=[WHOLE] * len(outs),
        scratch_shapes=list(scratch),
        cost_estimate=pl.CostEstimate(flops=0, bytes_accessed=0, transcendentals=0),
        compiler_params=pltpu.CompilerParams(vmem_limit_bytes=16 * 2**20),
        **kwargs,
    )(*operands, *later)


ANYWHERE = pl.BlockSpec(memory_space=pl.ANY)


def pair_kernel(token, cotangent, out, sems):
    copies = [
        pltpu.make_async_copy(value, out.at[:, pl.ds(place * 3072, 3072)], sems.at[place])
        for place, value in enumerate((token, cotangent))
    ]
    for copy in copies:
        copy.start()
    for copy in copies:
        copy.wait()


def weight_in_kernel(own, other, out, sem):
    copy = pltpu.make_async_copy(own, out.at[:, pl.ds(0, 384)], sem)
    copy.start()
    out[:, 384:] = other[...]
    copy.wait()


def weight_out_kernel(own, other, out, sem):
    copy = pltpu.make_async_copy(own, out.at[pl.ds(0, 384), :], sem)
    copy.start()
    out[384:, :] = other[...]
    copy.wait()


def rows16_kernel(own, other, out):
    out[...] = jnp.concatenate([own[...].astype(f32), other[...].astype(f32)], 0).astype(bf16)


def stack_kernel(*refs):
    start = 0
    for piece in refs[:-1]:
        refs[-1][pl.ds(start, piece.shape[0]), :] = piece[...]
        start += piece.shape[0]


def stack(pieces, later=()):
    rows = sum(piece.shape[0] for piece in pieces)
    return call(stack_kernel, [(rows, pieces[0].shape[1])], pieces, later)[0]


def halves_kernel(*refs):
    whole, top, bottom = refs[4:]
    stack_kernel(*refs[:4], whole)
    stack_kernel(*refs[:2], top)
    stack_kernel(*refs[2:4], bottom)


def partial_kernel(rows, weight_in, weight_out, *outs):
    outs, full = outs[:4], outs[4]
    quarter = rows.shape[0] // 4
    full[:, :768] = jnp.dot(rows[:, :3072], weight_in[...], preferred_element_type=f32).astype(bf16)
    full[:, 768:] = contract(rows[:, 3072:], weight_out[...], 1, 1).astype(bf16)
    me = lax.axis_index("inp")
    for step, out in zip((0, 2, 1, 3), outs):
        out[...] = full[pl.ds(pl.multiple_of(lax.rem(me + step, 4) * quarter, quarter), quarter), :]


def sum_inp(rows, weights, later=()):
    blocks = call(
        partial_kernel,
        [(rows.shape[0] // 4, 1536)] * 4,
        (rows, *weights),
        later,
        scratch=[pltpu.VMEM((rows.shape[0], 1536), bf16)],
    )
    return [blocks[0]] + [move_inp(block, step) for step, block in zip((2, 1, 3), blocks[1:])]


def gelu_kernel(*refs):
    own_act, other_act, grad_pre = refs[8:]
    start = 0
    for blocks in (refs[:4], refs[4:8]):
        total = sum(block[...].astype(f32) for block in blocks[1:]) + blocks[0][...].astype(f32)
        rows = pl.ds(start, total.shape[0])
        gelu_value, gelu_slope = gelu_parts(total[:, :768])
        own_act[rows, :] = gelu_value[:, :384].astype(bf16)
        other_act[rows, :] = gelu_value[:, 384:].astype(bf16)
        grad_pre[rows, :] = (total[:, 768:] * gelu_slope).astype(bf16)
        start += total.shape[0]


CHUNKS = ((0, 48), (48, 16))


def place_grad_kernel(*refs):
    out, sent = refs[4:]
    me = lax.axis_index("inp")
    for step, block in zip((0, 2, 1, 3), refs[:4]):
        place = lax.rem(me + step, 4)
        for start, rows in CHUNKS:
            to = pl.ds(pl.multiple_of(4 * start + place * rows, 16), rows)
            out[to, :] = block[start : start + rows, :]
            sent[to, :] = block[start : start + rows, 384:]


def place_act_kernel(*refs):
    me = lax.axis_index("inp")
    for step, block in zip((0, 2, 1, 3), refs[:4]):
        place = lax.rem(me + step, 4)
        for core in range(2):
            for start, rows in CHUNKS:
                to = pl.ds(pl.multiple_of(256 * core + 4 * start + place * rows, 16), rows)
                refs[4][to, :] = block[64 * core + start : 64 * core + start + rows, :]


def split_kernel(value, total, *blocks):
    total[...] = value[:64, :]
    for place, block in enumerate(blocks):
        block[...] = value[pl.ds(64 * place + 64, 64), :].astype(bf16)


def sum_kernel(own, first, second, third, total, *blocks):
    rows = total.shape[0]
    for place, out in enumerate((total, *blocks)):
        part = pl.ds(place * rows, rows)
        value = own[part, :] + first[part, :].astype(f32) + second[part, :].astype(f32) + third[part, :].astype(f32)
        out[...] = value.astype(out.dtype)


def last_kernel(own, first, second, third, total, sent):
    value = own[...] + first[...].astype(f32) + second[...].astype(f32) + third[...].astype(f32)
    total[...] = value[:8, :]
    sent[...] = value[8:, :].astype(bf16)


def copy_kernel(value, out):
    out[...] = value[...]


def after(value, *later):
    return call(copy_kernel, [value.shape], (value,), later)[0]


def shards(tokens, weight_in, weight_out, cotangent):
    dma = pltpu.SemaphoreType.DMA
    rows = call(
        pair_kernel, [(8, 6144)], (tokens, cotangent), in_specs=[ANYWHERE] * 2, scratch=[dma((2,))]
    )[0]
    rows_z = swap_z(rows)
    both = [ANYWHERE, WHOLE]
    weights = (
        call(weight_in_kernel, [(3072, 768)], (weight_in, swap_core(weight_in)), in_specs=both, scratch=[dma(())])[0],
        call(weight_out_kernel, [(768, 3072)], (weight_out, swap_core(weight_out)), in_specs=both, scratch=[dma(())])[0],
    )
    rows = call(rows16_kernel, [(16, 6144)], (rows, rows_z), weights)[0]
    rows, top, bottom = call(halves_kernel, [(64, 6144), (32, 6144), (32, 6144)], gather4(rows, 0))
    up = [move_chip(half, 1, -1) for half in (top, bottom)]
    down = [move_chip(half, 1, 1) for half in (top, bottom)]
    near_rows = stack((rows, *up, *down))
    far = [move_chip(up[0], 1, -1), move_chip(down[1], 1, 1)]
    near = sum_inp(near_rows, weights)
    far_rows = stack(far, near[:1])
    far = sum_inp(far_rows, weights)
    own_act, other_act, grad_pre = call(gelu_kernel, [(64, 384), (64, 384), (64, 768)], (*near, *far))
    act = stack((own_act, swap_core(other_act)))
    grad_pre, sent = call(
        place_grad_kernel, [(256, 768), (256, 384)], gather_inp(grad_pre), (act,)
    )
    total, *blocks = call(
        split_kernel,
        [jax.ShapeDtypeStruct((64, 3072), f32)] + [(64, 3072)] * 3,
        (contract(grad_pre, weights[0], 1, 1),),
    )
    own = stack((near_rows, far_rows), blocks[:1])
    other = swap_core(own)
    act = gather_inp(after(act, blocks[0]))
    grad_pre = (after(grad_pre, blocks[0])[:, :384], swap_core(after(sent, blocks[0])))
    total, *blocks = call(
        sum_kernel,
        [jax.ShapeDtypeStruct((16, 3072), f32)] + [(16, 3072)] * 3,
        (total, *scatter(blocks, 1, (1, 3, 2))),
        (grad_pre[1], act[1], act[2], other),
    )
    grad_weight_in = contract(own[:, :3072], grad_pre[0], 0, 0) + contract(other[:, :3072], grad_pre[1], 0, 0)
    grad_weight_in = grad_weight_in.astype(bf16)
    total, last = call(
        last_kernel,
        [jax.ShapeDtypeStruct((8, 3072), f32), (8, 3072)],
        (total, *scatter(blocks, 0, (2, 1, 3))),
        (grad_weight_in,),
    )
    grad_tokens = total + swap_z(last).astype(f32)
    act = call(place_act_kernel, [(512, 384)], act, (last,))[0]
    grad_weight_out = contract(act[:256], own[:, 3072:], 0, 0) + contract(act[256:], other[:, 3072:], 0, 0)
    return (grad_tokens.astype(bf16), grad_weight_in, grad_weight_out.astype(bf16))


def solution(mesh):
    in_specs = (
        P(("wt", "out"), "inp"),
        P("inp", ("wt", "out")),
        P(("wt", "out"), "inp"),
        P(("wt", "out"), "inp"),
    )
    out_specs = (P(("wt", "out"), "inp"), P("inp", ("wt", "out")), P(("wt", "out"), "inp"))
    return jax.shard_map(shards, mesh=mesh, in_specs=in_specs, out_specs=out_specs, check_vma=False)
```

time: 125 us -> 107 us (0.86); the launches traced: 125 us -> 105 us
  waiting for transfers between devices: 59.6 us -> 38 us
  Pallas kernels: 4.28 us -> 7.13 us
  local copies, waits for them, and re-layouts: 1.71 us -> 4.47 us
  matrix products: 8.58 us -> 6.54 us
  starting transfers between devices: 49.2 us -> 47.9 us
    ppermute x16 -> x22, waiting for transfers between devices: 41.8 us -> 19.3 us  [move(): return lax.ppermute(value, ('wt', 'out'), pairs)]
    ppermute x9 -> x12, starting transfers between devices: 18.3 us -> 14.4 us  [move_inp(): return lax.ppermute(value, 'inp', [(i, (i + step) % 4) for i in range(4)])]
    unnamed x8 -> x10, local copies, waits for them, and re-layouts: 1.6 us -> 4.47 us
    pallas_call x10 -> x20, Pallas kernels: 4.28 us -> 7.13 us  [call(): pl.pallas_call(body, out_shape=[out if isinstance(out, jax.ShapeDtypeStru...]
    ppermute x16 -> x22, starting transfers between devices: 30.9 us -> 33.5 us  [move(): return lax.ppermute(value, ('wt', 'out'), pairs)]
    dot_general x6 -> x5, matrix products: 8.58 us -> 6.54 us  [contract(): lax.dot_general(left, right, (((left_dim,), (right_dim,)), ((), ())), pre...]
    ppermute x9 -> x12, waiting for transfers between devices: 17.8 us -> 18.6 us  [move_inp(): return lax.ppermute(value, 'inp', [(i, (i + step) % 4) for i in range(4)])]
  transfers between devices with their start and end apart: 25 -> 34, of which waited for: 20 -> 18; matrix products, arithmetic and copies ran while one was open for 6% -> 5% of each run, Pallas kernels for 1% -> 6%
where the time goes in v3:
time: 107 us; the launch traced here: 105 us
  starting transfers between devices  47.9 us (45%)
  waiting for transfers between devices  38 us (36%)
  Pallas kernels  7.13 us (7%)
  matrix products  6.54 us (6%)
  local copies, waits for them, and re-layouts  4.47 us (4%)
    ppermute x22, starting transfers between devices, move(): return lax.ppermute(value, ('wt', 'out'), pairs)  33.5 us
    ppermute x22, waiting for transfers between devices, move(): return lax.ppermute(value, ('wt', 'out'), pairs)  19.3 us
    ppermute x12, waiting for transfers between devices, move_inp(): return lax.ppermute(value, 'inp', [(i, (i + step) % 4) for i in range(4)])  18.6 us
    ppermute x12, starting transfers between devices, move_inp(): return lax.ppermute(value, 'inp', [(i, (i + step) % 4) for i in range(4)])  14.4 us
    pallas_call x20, Pallas kernels, call(): pl.pallas_call(body, out_shape=[out if isinstance(out, jax.ShapeDtypeStru...  7.13 us
    dot_general x5, matrix products, contract(): lax.dot_general(left, right, (((left_dim,), (right_dim,)), ((), ())), pre...  6.54 us
    unnamed x10, local copies, waits for them, and re-layouts  4.47 us
  transfers between devices with their start and end apart: 34, of which 18 were waited for; matrix products, arithmetic and copies ran while one was open for 5% of the time, Pallas kernels for 6%

profile of v3, /device:TPU:2, one launch (start us, length us, event | category | flops | bytes accessed | tf_op | source)
XLA Modules:
  0.0 105.5 jit_solution(14160728185395916253)
XLA Ops:
  2.9 7.3 %collective-permute-start = (bf16[8,6144]{1,0:T(8,128)(2,1)S(1)}, bf16[8,6144]{1,0:T(8,128)(2,1)S(1)}, u32[]{:S(2)}, u32[]{:S(2)}) collective-permute-start(bf16[8,6144]{1,0:T(8,128)(2,1)S(1)} %shard_map.67.refs_0_), channel_id=1, source_target_pairs={{0,32},{1,33},{2,34},{3,35},{4,36},{5,37},{6,38},{7,39},{8,40},{9,... | collective-permute-start | bytes 294920 | tf_op jit(solution)/shard_map/ppermute | solution.py:38
  10.2 1.7 %copy-done.1 = bf16[3072,384]{1,0:T(8,128)(2,1)S(1)} copy-done((bf16[3072,384]{1,0:T(8,128)(2,1)S(1)}, bf16[3072,384]{1,0:T(8,128)(2,1)}, u32[]{:S(2)}) %copy-start.1) | copy-done | bytes 2359320
  13.9 3.3 %collective-permute-start.3 = (bf16[16,6144]{1,0:T(8,128)(2,1)S(1)}, bf16[16,6144]{1,0:T(8,128)(2,1)S(1)}, u32[]{:S(2)}, u32[]{:S(2)}) collective-permute-start(bf16[16,6144]{1,0:T(8,128)(2,1)S(1)} %shard_map.70.refs_0_), channel_id=1, source_target_pairs={{0,16},{1,5},{2,18},{3,7},{4,20},{5,1},{6,22},{7,3},{8,24},{9,13},... | collective-permute-start | bytes 589832 | tf_op jit(solution)/shard_map/ppermute | solution.py:38
  19.2 2.0 %collective-permute-done.3.refs_1_ = bf16[16,6144]{1,0:T(8,128)(2,1)S(1)} collective-permute-done((bf16[16,6144]{1,0:T(8,128)(2,1)S(1)}, bf16[16,6144]{1,0:T(8,128)(2,1)S(1)}, u32[]{:S(2)}, u32[]{:S(2)}) %collective-permute-start.3) | collective-permute-done | bytes 196640 | tf_op jit(solution)/shard_map/ppermute | solution.py:38
  21.2 2.4 %collective-permute-done.4.refs_2_ = bf16[16,6144]{1,0:T(8,128)(2,1)S(1)} collective-permute-done((bf16[16,6144]{1,0:T(8,128)(2,1)S(1)}, bf16[16,6144]{1,0:T(8,128)(2,1)S(1)}, u32[]{:S(2)}, u32[]{:S(2)}) %collective-permute-start.4) | collective-permute-done | bytes 196640 | tf_op jit(solution)/shard_map/ppermute | solution.py:38
  29.4 3.7 %collective-permute-done.6.refs_1_ = bf16[32,6144]{1,0:T(8,128)(2,1)S(1)} collective-permute-done((bf16[32,6144]{1,0:T(8,128)(2,1)S(1)}, bf16[32,6144]{1,0:T(8,128)(2,1)S(1)}, u32[]{:S(2)}, u32[]{:S(2)}) %collective-permute-start.6) | collective-permute-done | bytes 393248 | tf_op jit(solution)/shard_map/ppermute | solution.py:38
  35.1 2.2 %collective-permute-done.7.refs_2_ = bf16[32,6144]{1,0:T(8,128)(2,1)S(1)} collective-permute-done((bf16[32,6144]{1,0:T(8,128)(2,1)S(1)}, bf16[32,6144]{1,0:T(8,128)(2,1)S(1)}, u32[]{:S(2)}, u32[]{:S(2)}) %collective-permute-start.7) | collective-permute-done | bytes 393248 | tf_op jit(solution)/shard_map/ppermute | solution.py:38
  38.7 2.6 %shard_map.73 = (bf16[48,1536]{1,0:T(8,128)(2,1)S(1)}, bf16[48,1536]{1,0:T(8,128)(2,1)S(1)}, bf16[48,1536]{1,0:T(8,128)(2,1)S(1)}, bf16[48,1536]{1,0:T(8,128)(2,1)S(1)}) custom-call(bf16[192,6144]{1,0:T(8,128)(2,1)S(1)} %shard_map.72.refs_0_, bf16[3072,768]{1,0:T(8,128)(2,1)S(1)} %shard_map.68.refs_2_.refs_1_, bf16[768,3072]{1,0:T(8,128)(2,1)S(1)} %shard_map.69.refs_3_.refs_2_), custom_call_target="tpu_custom_call" | custom-call | tf_op jit(solution)/shard_map/pallas_call | solution.py:81
  41.3 3.5 %collective-permute-start.10 = (bf16[48,1536]{1,0:T(8,128)(2,1)S(1)}, bf16[48,1536]{1,0:T(8,128)(2,1)S(1)}, u32[]{:S(2)}, u32[]{:S(2)}) collective-permute-start(bf16[48,1536]{1,0:T(8,128)(2,1)S(1)} %get-tuple-element.33), channel_id=1, source_target_pairs={{0,128},{64,192},{128,0},{192,64},{1,129},{65,193},{129,1},{193,65... | collective-permute-start | bytes 442376 | tf_op jit(solution)/shard_map/ppermute | solution.py:66
  44.8 3.8 %collective-permute-start.12 = (bf16[48,1536]{1,0:T(8,128)(2,1)S(1)}, bf16[48,1536]{1,0:T(8,128)(2,1)S(1)}, u32[]{:S(2)}, u32[]{:S(2)}) collective-permute-start(bf16[48,1536]{1,0:T(8,128)(2,1)S(1)} %get-tuple-element.35), channel_id=1, source_target_pairs={{0,192},{64,0},{128,64},{192,128},{1,193},{65,1},{129,65},{193,129... | collective-permute-start | bytes 442376 | tf_op jit(solution)/shard_map/ppermute | solution.py:66
  48.7 2.3 %shard_map.75 = (bf16[16,1536]{1,0:T(8,128)(2,1)S(1)}, bf16[16,1536]{1,0:T(8,128)(2,1)S(1)}, bf16[16,1536]{1,0:T(8,128)(2,1)S(1)}, bf16[16,1536]{1,0:T(8,128)(2,1)S(1)}) custom-call(bf16[64,6144]{1,0:T(8,128)(2,1)S(1)} %shard_map.74.refs_0_.refs_1_, bf16[3072,768]{1,0:T(8,128)(2,1)S(1)} %shard_map.68.refs_2_.refs_1_, ...), custom_call_target="tpu_custom_call" | custom-call | tf_op jit(solution)/shard_map/pallas_call | solution.py:81
  51.7 3.7 %collective-permute-done.10.refs_1_ = bf16[48,1536]{1,0:T(8,128)(2,1)S(1)} collective-permute-done((bf16[48,1536]{1,0:T(8,128)(2,1)S(1)}, bf16[48,1536]{1,0:T(8,128)(2,1)S(1)}, u32[]{:S(2)}, u32[]{:S(2)}) %collective-permute-start.10) | collective-permute-done | bytes 147488 | tf_op jit(solution)/shard_map/ppermute | solution.py:66
  55.9 4.2 %collective-permute-done.15.refs_5_ = bf16[16,1536]{1,0:T(8,128)(2,1)S(1)} collective-permute-done((bf16[16,1536]{1,0:T(8,128)(2,1)S(1)}, bf16[16,1536]{1,0:T(8,128)(2,1)S(1)}, u32[]{:S(2)}, u32[]{:S(2)}) %collective-permute-start.15) | collective-permute-done | bytes 49184 | tf_op jit(solution)/shard_map/ppermute | solution.py:66
  61.8 2.1 %collective-permute-start.19 = (bf16[64,768]{1,0:T(8,128)(2,1)S(1)}, bf16[64,768]{1,0:T(8,128)(2,1)S(1)}, u32[]{:S(2)}, u32[]{:S(2)}) collective-permute-start(bf16[64,768]{1,0:T(8,128)(2,1)S(1)} %get-tuple-element.40.refs_0_), channel_id=1, source_target_pairs={{0,192},{64,0},{128,64},{192,128},{1,193},{65,1},{129,65},{193,129... | collective-permute-start | bytes 294920 | tf_op jit(solution)/shard_map/ppermute | solution.py:66
  65.1 3.0 %collective-permute-done.18.refs_1_ = bf16[64,768]{1,0:T(8,128)(2,1)S(1)} collective-permute-done((bf16[64,768]{1,0:T(8,128)(2,1)S(1)}, bf16[64,768]{1,0:T(8,128)(2,1)S(1)}, u32[]{:S(2)}, u32[]{:S(2)}) %collective-permute-start.18) | collective-permute-done | bytes 98336 | tf_op jit(solution)/shard_map/ppermute | solution.py:66
  68.1 2.2 %collective-permute-done.20.refs_3_ = bf16[64,768]{1,0:T(8,128)(2,1)S(1)} collective-permute-done((bf16[64,768]{1,0:T(8,128)(2,1)S(1)}, bf16[64,768]{1,0:T(8,128)(2,1)S(1)}, u32[]{:S(2)}, u32[]{:S(2)}) %collective-permute-start.20) | collective-permute-done | bytes 98336 | tf_op jit(solution)/shard_map/ppermute | solution.py:66
  73.4 2.1 %collective-permute-start.22 = (bf16[64,3072]{1,0:T(8,128)(2,1)S(1)}, bf16[64,3072]{1,0:T(8,128)(2,1)S(1)}, u32[]{:S(2)}, u32[]{:S(2)}) collective-permute-start(bf16[64,3072]{1,0:T(8,128)(2,1)S(1)} %get-tuple-element.45.refs_1_.refs_2_), channel_id=1, source_target_pairs={{0,2},{1,9},{2,4},{3,11},{4,6},{5,13},{6,0},{7,15},{8,10},{9,17},{... | collective-permute-start | bytes 1179656 | tf_op jit(solution)/shard_map/ppermute | solution.py:38
  76.3 2.1 %collective-permute-start.24 = (bf16[64,3072]{1,0:T(8,128)(2,1)S(1)}, bf16[64,3072]{1,0:T(8,128)(2,1)S(1)}, u32[]{:S(2)}, u32[]{:S(2)}) collective-permute-start(bf16[64,3072]{1,0:T(8,128)(2,1)S(1)} %get-tuple-element.47), channel_id=1, source_target_pairs={{0,4},{1,17},{2,6},{3,19},{4,0},{5,21},{6,2},{7,23},{8,12},{9,25},... | collective-permute-start | bytes 1179656 | tf_op jit(solution)/shard_map/ppermute | solution.py:38
  78.3 2.3 %collective-permute-done.26.refs_5_.refs_1_ = bf16[128,384]{1,0:T(8,128)(2,1)S(1)} collective-permute-done((bf16[128,384]{1,0:T(8,128)(2,1)S(1)}, bf16[128,384]{1,0:T(8,128)(2,1)S(1)}, u32[]{:S(2)}, u32[]{:S(2)}) %collective-permute-start.26) | collective-permute-done | bytes 98336 | tf_op jit(solution)/shard_map/ppermute | solution.py:66
  82.0 3.2 %collective-permute-done.27.refs_6_.refs_2_ = bf16[128,384]{1,0:T(8,128)(2,1)S(1)} collective-permute-done((bf16[128,384]{1,0:T(8,128)(2,1)S(1)}, bf16[128,384]{1,0:T(8,128)(2,1)S(1)}, u32[]{:S(2)}, u32[]{:S(2)}) %collective-permute-start.27) | collective-permute-done | bytes 98336 | tf_op jit(solution)/shard_map/ppermute | solution.py:66
  88.6 1.7 %collective-permute-start.30 = (bf16[16,3072]{1,0:T(8,128)(2,1)S(1)}, bf16[16,3072]{1,0:T(8,128)(2,1)S(1)}, u32[]{:S(2)}, u32[]{:S(2)}) collective-permute-start(bf16[16,3072]{1,0:T(8,128)(2,1)S(1)} %get-tuple-element.51), channel_id=1, source_target_pairs={{0,8},{1,3},{2,10},{3,5},{4,12},{5,7},{6,14},{7,1},{8,16},{9,11},{... | collective-permute-start | bytes 294920 | tf_op jit(solution)/shard_map/ppermute | solution.py:38
  90.2 1.6 %collective-permute-start.31 = (bf16[16,3072]{1,0:T(8,128)(2,1)S(1)}, bf16[16,3072]{1,0:T(8,128)(2,1)S(1)}, u32[]{:S(2)}, u32[]{:S(2)}) collective-permute-start(bf16[16,3072]{1,0:T(8,128)(2,1)S(1)} %get-tuple-element.52), channel_id=1, source_target_pairs={{0,24},{1,7},{2,26},{3,1},{4,28},{5,3},{6,30},{7,5},{8,0},{9,15},{... | collective-permute-start | bytes 294920 | tf_op jit(solution)/shard_map/ppermute | solution.py:38
  95.6 6.1 %collective-permute-start.32 = (bf16[8,3072]{1,0:T(8,128)(2,1)S(1)}, bf16[8,3072]{1,0:T(8,128)(2,1)S(1)}, u32[]{:S(2)}, u32[]{:S(2)}) collective-permute-start(bf16[8,3072]{1,0:T(8,128)(2,1)S(1)} %get-tuple-element.54.refs_4_), channel_id=1, source_target_pairs={{0,32},{1,33},{2,34},{3,35},{4,36},{5,37},{6,38},{7,39},{8,40},{9,... | collective-permute-start | bytes 147464 | tf_op jit(solution)/shard_map/ppermute | solution.py:38
  102.6 2.2 %add_convert_fusion = bf16[384,3072]{1,0:T(8,128)(2,1)} fusion(f32[384,3072]{1,0:T(8,128)S(1)} %fusion, bf16[256,6144]{1,0:T(8,128)(2,1)S(1)} %shard_map.82, bf16[512,384]{1,0:T(8,128)(2,1)S(1)} %shard_map.86), kind=kOutput, calls=%fused_computation | convolution fusion | flops 606339072 | bytes 8847360 | tf_op jit(solution)/shard_map/dot_general | solution.py:25
  (80 shorter events, 33.3 us)
Async XLA Ops:
  0.6 9.6 %collective-permute-start.1 = (bf16[3072,384]{1,0:T(8,128)(2,1)}, bf16[3072,384]{1,0:T(8,128)(2,1)S(1)}, u32[]{:S(2)}, u32[]{:S(2)}) collective-permute-start(bf16[3072,384]{1,0:T(8,128)(2,1)} %refs_0_.4), channel_id=1, source_target_pairs={{0,1},{1,0},{2,3},{3,2},{4,5},{5,4},{6,7},{7,6},{8,9},{9,8},{10,11... | collective-permute-start | bytes 7077896 | tf_op jit(solution)/shard_map/ppermute | solution.py:38
  0.7 11.6 %collective-permute-start.2 = (bf16[384,3072]{1,0:T(8,128)(2,1)}, bf16[384,3072]{1,0:T(8,128)(2,1)S(1)}, u32[]{:S(2)}, u32[]{:S(2)}) collective-permute-start(bf16[384,3072]{1,0:T(8,128)(2,1)} %refs_0_.5), channel_id=1, source_target_pairs={{0,1},{1,0},{2,3},{3,2},{4,5},{5,4},{6,7},{7,6},{8,9},{9,8},{10,11... | collective-permute-start | bytes 7077896 | tf_op jit(solution)/shard_map/ppermute | solution.py:38
  2.9 10.9 %collective-permute-start = (bf16[8,6144]{1,0:T(8,128)(2,1)S(1)}, bf16[8,6144]{1,0:T(8,128)(2,1)S(1)}, u32[]{:S(2)}, u32[]{:S(2)}) collective-permute-start(bf16[8,6144]{1,0:T(8,128)(2,1)S(1)} %shard_map.67.refs_0_), channel_id=1, source_target_pairs={{0,32},{1,33},{2,34},{3,35},{4,36},{5,37},{6,38},{7,39},{8,40},{9,... | collective-permute-start | bytes 294920 | tf_op jit(solution)/shard_map/ppermute | solution.py:38
  13.9 7.3 %collective-permute-start.3 = (bf16[16,6144]{1,0:T(8,128)(2,1)S(1)}, bf16[16,6144]{1,0:T(8,128)(2,1)S(1)}, u32[]{:S(2)}, u32[]{:S(2)}) collective-permute-start(bf16[16,6144]{1,0:T(8,128)(2,1)S(1)} %shard_map.70.refs_0_), channel_id=1, source_target_pairs={{0,16},{1,5},{2,18},{3,7},{4,20},{5,1},{6,22},{7,3},{8,24},{9,13},... | collective-permute-start | bytes 589832 | tf_op jit(solution)/shard_map/ppermute | solution.py:38
  25.2 7.9 %collective-permute-start.6 = (bf16[32,6144]{1,0:T(8,128)(2,1)S(1)}, bf16[32,6144]{1,0:T(8,128)(2,1)S(1)}, u32[]{:S(2)}, u32[]{:S(2)}) collective-permute-start(bf16[32,6144]{1,0:T(8,128)(2,1)S(1)} %get-tuple-element.30), channel_id=1, source_target_pairs={{0,6},{1,25},{2,0},{3,27},{4,2},{5,29},{6,4},{7,31},{8,14},{9,1},{... | collective-permute-start | bytes 1179656 | tf_op jit(solution)/shard_map/ppermute | solution.py:38
  25.9 8.5 %collective-permute-start.9 = (bf16[32,6144]{1,0:T(8,128)(2,1)S(1)}, bf16[32,6144]{1,0:T(8,128)(2,1)S(1)}, u32[]{:S(2)}, u32[]{:S(2)}) collective-permute-start(bf16[32,6144]{1,0:T(8,128)(2,1)S(1)} %get-tuple-element.31), channel_id=1, source_target_pairs={{0,2},{1,9},{2,4},{3,11},{4,6},{5,13},{6,0},{7,15},{8,10},{9,17},{... | collective-permute-start | bytes 1179656 | tf_op jit(solution)/shard_map/ppermute | solution.py:38
  27.3 10.0 %collective-permute-start.7 = (bf16[32,6144]{1,0:T(8,128)(2,1)S(1)}, bf16[32,6144]{1,0:T(8,128)(2,1)S(1)}, u32[]{:S(2)}, u32[]{:S(2)}) collective-permute-start(bf16[32,6144]{1,0:T(8,128)(2,1)S(1)} %get-tuple-element.31), channel_id=1, source_target_pairs={{0,6},{1,25},{2,0},{3,27},{4,2},{5,29},{6,4},{7,31},{8,14},{9,1},{... | collective-permute-start | bytes 1179656 | tf_op jit(solution)/shard_map/ppermute | solution.py:38
  28.6 10.0 %collective-permute-start.8 = (bf16[32,6144]{1,0:T(8,128)(2,1)S(1)}, bf16[32,6144]{1,0:T(8,128)(2,1)S(1)}, u32[]{:S(2)}, u32[]{:S(2)}) collective-permute-start(bf16[32,6144]{1,0:T(8,128)(2,1)S(1)} %get-tuple-element.30), channel_id=1, source_target_pairs={{0,2},{1,9},{2,4},{3,11},{4,6},{5,13},{6,0},{7,15},{8,10},{9,17},{... | collective-permute-start | bytes 1179656 | tf_op jit(solution)/shard_map/ppermute | solution.py:38
  33.1 15.5 %collective-permute-start.13 = (bf16[32,6144]{1,0:T(8,128)(2,1)S(1)}, bf16[32,6144]{1,0:T(8,128)(2,1)S(1)}, u32[]{:S(2)}, u32[]{:S(2)}) collective-permute-start(bf16[32,6144]{1,0:T(8,128)(2,1)S(1)} %collective-permute-done.6.refs_1_), channel_id=1, source_target_pairs={{0,6},{1,25},{2,0},{3,27},{4,2},{5,29},{6,4},{7,31},{8,14},{9,1},{... | collective-permute-start | bytes 1179656 | tf_op jit(solution)/shard_map/ppermute | solution.py:38
  34.4 14.3 %collective-permute-start.14 = (bf16[32,6144]{1,0:T(8,128)(2,1)S(1)}, bf16[32,6144]{1,0:T(8,128)(2,1)S(1)}, u32[]{:S(2)}, u32[]{:S(2)}) collective-permute-start(bf16[32,6144]{1,0:T(8,128)(2,1)S(1)} %collective-permute-done.9.refs_4_), channel_id=1, source_target_pairs={{0,2},{1,9},{2,4},{3,11},{4,6},{5,13},{6,0},{7,15},{8,10},{9,17},{... | collective-permute-start | bytes 1179656 | tf_op jit(solution)/shard_map/ppermute | solution.py:38
  41.3 14.0 %collective-permute-start.10 = (bf16[48,1536]{1,0:T(8,128)(2,1)S(1)}, bf16[48,1536]{1,0:T(8,128)(2,1)S(1)}, u32[]{:S(2)}, u32[]{:S(2)}) collective-permute-start(bf16[48,1536]{1,0:T(8,128)(2,1)S(1)} %get-tuple-element.33), channel_id=1, source_target_pairs={{0,128},{64,192},{128,0},{192,64},{1,129},{65,193},{129,1},{193,65... | collective-permute-start | bytes 442376 | tf_op jit(solution)/shard_map/ppermute | solution.py:66
  44.8 11.1 %collective-permute-start.11 = (bf16[48,1536]{1,0:T(8,128)(2,1)S(1)}, bf16[48,1536]{1,0:T(8,128)(2,1)S(1)}, u32[]{:S(2)}, u32[]{:S(2)}) collective-permute-start(bf16[48,1536]{1,0:T(8,128)(2,1)S(1)} %get-tuple-element.34), channel_id=1, source_target_pairs={{0,64},{64,128},{128,192},{192,0},{1,65},{65,129},{129,193},{193,1... | collective-permute-start | bytes 442376 | tf_op jit(solution)/shard_map/ppermute | solution.py:66
  44.8 11.1 %collective-permute-start.12 = (bf16[48,1536]{1,0:T(8,128)(2,1)S(1)}, bf16[48,1536]{1,0:T(8,128)(2,1)S(1)}, u32[]{:S(2)}, u32[]{:S(2)}) collective-permute-start(bf16[48,1536]{1,0:T(8,128)(2,1)S(1)} %get-tuple-element.35), channel_id=1, source_target_pairs={{0,192},{64,0},{128,64},{192,128},{1,193},{65,1},{129,65},{193,129... | collective-permute-start | bytes 442376 | tf_op jit(solution)/shard_map/ppermute | solution.py:66
  51.0 9.1 %collective-permute-start.15 = (bf16[16,1536]{1,0:T(8,128)(2,1)S(1)}, bf16[16,1536]{1,0:T(8,128)(2,1)S(1)}, u32[]{:S(2)}, u32[]{:S(2)}) collective-permute-start(bf16[16,1536]{1,0:T(8,128)(2,1)S(1)} %get-tuple-element.37), channel_id=1, source_target_pairs={{0,128},{64,192},{128,0},{192,64},{1,129},{65,193},{129,1},{193,65... | collective-permute-start | bytes 147464 | tf_op jit(solution)/shard_map/ppermute | solution.py:66
  51.1 9.0 %collective-permute-start.16 = (bf16[16,1536]{1,0:T(8,128)(2,1)S(1)}, bf16[16,1536]{1,0:T(8,128)(2,1)S(1)}, u32[]{:S(2)}, u32[]{:S(2)}) collective-permute-start(bf16[16,1536]{1,0:T(8,128)(2,1)S(1)} %get-tuple-element.38), channel_id=1, source_target_pairs={{0,64},{64,128},{128,192},{192,0},{1,65},{65,129},{129,193},{193,1... | collective-permute-start | bytes 147464 | tf_op jit(solution)/shard_map/ppermute | solution.py:66
  60.3 7.8 %collective-permute-start.18 = (bf16[64,768]{1,0:T(8,128)(2,1)S(1)}, bf16[64,768]{1,0:T(8,128)(2,1)S(1)}, u32[]{:S(2)}, u32[]{:S(2)}) collective-permute-start(bf16[64,768]{1,0:T(8,128)(2,1)S(1)} %get-tuple-element.40.refs_0_), channel_id=1, source_target_pairs={{0,128},{64,192},{128,0},{192,64},{1,129},{65,193},{129,1},{193,65... | collective-permute-start | bytes 294920 | tf_op jit(solution)/shard_map/ppermute | solution.py:66
  72.2 16.1 %collective-permute-start.28 = (bf16[256,6144]{1,0:T(8,128)(2,1)S(1)}, bf16[256,6144]{1,0:T(8,128)(2,1)S(1)}, u32[]{:S(2)}, u32[]{:S(2)}) collective-permute-start(bf16[256,6144]{1,0:T(8,128)(2,1)S(1)} %shard_map.82), channel_id=1, source_target_pairs={{0,1},{1,0},{2,3},{3,2},{4,5},{5,4},{6,7},{7,6},{8,9},{9,8},{10,11... | collective-permute-start | bytes 9437192 | tf_op jit(solution)/shard_map/ppermute | solution.py:38
  72.3 8.3 %collective-permute-start.26 = (bf16[128,384]{1,0:T(8,128)(2,1)S(1)}, bf16[128,384]{1,0:T(8,128)(2,1)S(1)}, u32[]{:S(2)}, u32[]{:S(2)}) collective-permute-start(bf16[128,384]{1,0:T(8,128)(2,1)S(1)} %shard_map.81.refs_0_), channel_id=1, source_target_pairs={{0,128},{64,192},{128,0},{192,64},{1,129},{65,193},{129,1},{193,65... | collective-permute-start | bytes 294920 | tf_op jit(solution)/shard_map/ppermute | solution.py:66
  73.4 13.3 %collective-permute-start.22 = (bf16[64,3072]{1,0:T(8,128)(2,1)S(1)}, bf16[64,3072]{1,0:T(8,128)(2,1)S(1)}, u32[]{:S(2)}, u32[]{:S(2)}) collective-permute-start(bf16[64,3072]{1,0:T(8,128)(2,1)S(1)} %get-tuple-element.45.refs_1_.refs_2_), channel_id=1, source_target_pairs={{0,2},{1,9},{2,4},{3,11},{4,6},{5,13},{6,0},{7,15},{8,10},{9,17},{... | collective-permute-start | bytes 1179656 | tf_op jit(solution)/shard_map/ppermute | solution.py:38
  75.5 11.2 %collective-permute-start.23 = (bf16[64,3072]{1,0:T(8,128)(2,1)S(1)}, bf16[64,3072]{1,0:T(8,128)(2,1)S(1)}, u32[]{:S(2)}, u32[]{:S(2)}) collective-permute-start(bf16[64,3072]{1,0:T(8,128)(2,1)S(1)} %get-tuple-element.46), channel_id=1, source_target_pairs={{0,6},{1,25},{2,0},{3,27},{4,2},{5,29},{6,4},{7,31},{8,14},{9,1},{... | collective-permute-start | bytes 1179656 | tf_op jit(solution)/shard_map/ppermute | solution.py:38
  76.3 12.0 %collective-permute-start.24 = (bf16[64,3072]{1,0:T(8,128)(2,1)S(1)}, bf16[64,3072]{1,0:T(8,128)(2,1)S(1)}, u32[]{:S(2)}, u32[]{:S(2)}) collective-permute-start(bf16[64,3072]{1,0:T(8,128)(2,1)S(1)} %get-tuple-element.47), channel_id=1, source_target_pairs={{0,4},{1,17},{2,6},{3,19},{4,0},{5,21},{6,2},{7,23},{8,12},{9,25},... | collective-permute-start | bytes 1179656 | tf_op jit(solution)/shard_map/ppermute | solution.py:38
  86.7 15.0 %collective-permute-start.33 = (bf16[128,384]{1,0:T(8,128)(2,1)S(1)}, bf16[128,384]{1,0:T(8,128)(2,1)S(1)}, u32[]{:S(2)}, u32[]{:S(2)}) collective-permute-start(bf16[128,384]{1,0:T(8,128)(2,1)S(1)} %shard_map.81.refs_0_), channel_id=1, source_target_pairs={{0,64},{64,128},{128,192},{192,0},{1,65},{65,129},{129,193},{193,1... | collective-permute-start | bytes 294920 | tf_op jit(solution)/shard_map/ppermute | solution.py:66
  88.6 7.0 %collective-permute-start.30 = (bf16[16,3072]{1,0:T(8,128)(2,1)S(1)}, bf16[16,3072]{1,0:T(8,128)(2,1)S(1)}, u32[]{:S(2)}, u32[]{:S(2)}) collective-permute-start(bf16[16,3072]{1,0:T(8,128)(2,1)S(1)} %get-tuple-element.51), channel_id=1, source_target_pairs={{0,8},{1,3},{2,10},{3,5},{4,12},{5,7},{6,14},{7,1},{8,16},{9,11},{... | collective-permute-start | bytes 294920 | tf_op jit(solution)/shard_map/ppermute | solution.py:38
  95.6 9.3 %collective-permute-start.32 = (bf16[8,3072]{1,0:T(8,128)(2,1)S(1)}, bf16[8,3072]{1,0:T(8,128)(2,1)S(1)}, u32[]{:S(2)}, u32[]{:S(2)}) collective-permute-start(bf16[8,3072]{1,0:T(8,128)(2,1)S(1)} %get-tuple-element.54.refs_4_), channel_id=1, source_target_pairs={{0,32},{1,33},{2,34},{3,35},{4,36},{5,37},{6,38},{7,39},{8,40},{9,... | collective-permute-start | bytes 147464 | tf_op jit(solution)/shard_map/ppermute | solution.py:38
  (15 other events, 63.2 us)

commit v4 on v3

--- a/solution.py
+++ b/solution.py
@@ -265,7 +265,7 @@
         sum_kernel,
         [jax.ShapeDtypeStruct((16, 3072), f32)] + [(16, 3072)] * 3,
         (total, *scatter(blocks, 1, (1, 3, 2))),
-        (grad_pre[1], act[1], act[2], other),
+        (grad_pre[1], other),
     )
     grad_weight_in = contract(own[:, :3072], grad_pre[0], 0, 0) + contract(other[:, :3072], grad_pre[1], 0, 0)
     grad_weight_in = grad_weight_in.astype(bf16)

time: 107 us -> 111 us (1.037)
  waiting for transfers between devices: 38 us -> 40.1 us
  starting transfers between devices: 47.9 us -> 49.3 us
    ppermute x22, waiting for transfers between devices: 19.3 us -> 27 us  [move(): return lax.ppermute(value, ('wt', 'out'), pairs)]
    ppermute x12, waiting for transfers between devices: 18.6 us -> 13.1 us  [move_inp(): return lax.ppermute(value, 'inp', [(i, (i + step) % 4) for i in range(4)])]
    ppermute x12, starting transfers between devices: 14.4 us -> 15.6 us  [move_inp(): return lax.ppermute(value, 'inp', [(i, (i + step) % 4) for i in range(4)])]
  transfers between devices with their start and end apart: 34 -> 34, of which waited for: 18 -> 17; matrix products, arithmetic and copies ran while one was open for 5% -> 5% of each run, Pallas kernels for 6% -> 6%
where the time goes in v4:
time: 111 us; the launch traced here: 109 us
  starting transfers between devices  49.3 us (44%)
  waiting for transfers between devices  40.1 us (36%)
  Pallas kernels  7.13 us (6%)
  matrix products  6.49 us (6%)
  local copies, waits for them, and re-layouts  4.47 us (4%)
    ppermute x22, starting transfers between devices, move(): return lax.ppermute(value, ('wt', 'out'), pairs)  33.7 us
    ppermute x22, waiting for transfers between devices, move(): return lax.ppermute(value, ('wt', 'out'), pairs)  27 us
    ppermute x12, starting transfers between devices, move_inp(): return lax.ppermute(value, 'inp', [(i, (i + step) % 4) for i in range(4)])  15.6 us
    ppermute x12, waiting for transfers between devices, move_inp(): return lax.ppermute(value, 'inp', [(i, (i + step) % 4) for i in range(4)])  13.1 us
    pallas_call x20, Pallas kernels, call(): pl.pallas_call(body, out_shape=[out if isinstance(out, jax.ShapeDtypeStru...  7.13 us
    dot_general x5, matrix products, contract(): lax.dot_general(left, right, (((left_dim,), (right_dim,)), ((), ())), pre...  6.49 us
    unnamed x10, local copies, waits for them, and re-layouts  4.47 us
  transfers between devices with their start and end apart: 34, of which 17 were waited for; matrix products, arithmetic and copies ran while one was open for 5% of the time, Pallas kernels for 6%

profile of v4, /device:TPU:2, one launch (start us, length us, event | category | flops | bytes accessed | tf_op | source)
XLA Modules:
  0.0 109.1 jit_solution(3782194916991956608)
XLA Ops:
  2.9 7.3 %collective-permute-start = (bf16[8,6144]{1,0:T(8,128)(2,1)S(1)}, bf16[8,6144]{1,0:T(8,128)(2,1)S(1)}, u32[]{:S(2)}, u32[]{:S(2)}) collective-permute-start(bf16[8,6144]{1,0:T(8,128)(2,1)S(1)} %shard_map.67.refs_0_), channel_id=1, source_target_pairs={{0,32},{1,33},{2,34},{3,35},{4,36},{5,37},{6,38},{7,39},{8,40},{9,... | collective-permute-start | bytes 294920 | tf_op jit(solution)/shard_map/ppermute | solution.py:38
  13.9 3.3 %collective-permute-start.3 = (bf16[16,6144]{1,0:T(8,128)(2,1)S(1)}, bf16[16,6144]{1,0:T(8,128)(2,1)S(1)}, u32[]{:S(2)}, u32[]{:S(2)}) collective-permute-start(bf16[16,6144]{1,0:T(8,128)(2,1)S(1)} %shard_map.70.refs_0_), channel_id=1, source_target_pairs={{0,16},{1,5},{2,18},{3,7},{4,20},{5,1},{6,22},{7,3},{8,24},{9,13},... | collective-permute-start | bytes 589832 | tf_op jit(solution)/shard_map/ppermute | solution.py:38
  19.2 2.0 %collective-permute-done.3.refs_1_ = bf16[16,6144]{1,0:T(8,128)(2,1)S(1)} collective-permute-done((bf16[16,6144]{1,0:T(8,128)(2,1)S(1)}, bf16[16,6144]{1,0:T(8,128)(2,1)S(1)}, u32[]{:S(2)}, u32[]{:S(2)}) %collective-permute-start.3) | collective-permute-done | bytes 196640 | tf_op jit(solution)/shard_map/ppermute | solution.py:38
  21.2 2.4 %collective-permute-done.4.refs_2_ = bf16[16,6144]{1,0:T(8,128)(2,1)S(1)} collective-permute-done((bf16[16,6144]{1,0:T(8,128)(2,1)S(1)}, bf16[16,6144]{1,0:T(8,128)(2,1)S(1)}, u32[]{:S(2)}, u32[]{:S(2)}) %collective-permute-start.4) | collective-permute-done | bytes 196640 | tf_op jit(solution)/shard_map/ppermute | solution.py:38
  29.4 3.7 %collective-permute-done.6.refs_1_ = bf16[32,6144]{1,0:T(8,128)(2,1)S(1)} collective-permute-done((bf16[32,6144]{1,0:T(8,128)(2,1)S(1)}, bf16[32,6144]{1,0:T(8,128)(2,1)S(1)}, u32[]{:S(2)}, u32[]{:S(2)}) %collective-permute-start.6) | collective-permute-done | bytes 393248 | tf_op jit(solution)/shard_map/ppermute | solution.py:38
  35.1 2.2 %collective-permute-done.7.refs_2_ = bf16[32,6144]{1,0:T(8,128)(2,1)S(1)} collective-permute-done((bf16[32,6144]{1,0:T(8,128)(2,1)S(1)}, bf16[32,6144]{1,0:T(8,128)(2,1)S(1)}, u32[]{:S(2)}, u32[]{:S(2)}) %collective-permute-start.7) | collective-permute-done | bytes 393248 | tf_op jit(solution)/shard_map/ppermute | solution.py:38
  38.7 2.6 %shard_map.73 = (bf16[48,1536]{1,0:T(8,128)(2,1)S(1)}, bf16[48,1536]{1,0:T(8,128)(2,1)S(1)}, bf16[48,1536]{1,0:T(8,128)(2,1)S(1)}, bf16[48,1536]{1,0:T(8,128)(2,1)S(1)}) custom-call(bf16[192,6144]{1,0:T(8,128)(2,1)S(1)} %shard_map.72.refs_0_, bf16[3072,768]{1,0:T(8,128)(2,1)S(1)} %shard_map.68.refs_2_.refs_1_, bf16[768,3072]{1,0:T(8,128)(2,1)S(1)} %shard_map.69.refs_3_.refs_2_), custom_call_target="tpu_custom_call" | custom-call | tf_op jit(solution)/shard_map/pallas_call | solution.py:81
  41.3 3.5 %collective-permute-start.10 = (bf16[48,1536]{1,0:T(8,128)(2,1)S(1)}, bf16[48,1536]{1,0:T(8,128)(2,1)S(1)}, u32[]{:S(2)}, u32[]{:S(2)}) collective-permute-start(bf16[48,1536]{1,0:T(8,128)(2,1)S(1)} %get-tuple-element.33), channel_id=1, source_target_pairs={{0,128},{64,192},{128,0},{192,64},{1,129},{65,193},{129,1},{193,65... | collective-permute-start | bytes 442376 | tf_op jit(solution)/shard_map/ppermute | solution.py:66
  44.8 3.8 %collective-permute-start.12 = (bf16[48,1536]{1,0:T(8,128)(2,1)S(1)}, bf16[48,1536]{1,0:T(8,128)(2,1)S(1)}, u32[]{:S(2)}, u32[]{:S(2)}) collective-permute-start(bf16[48,1536]{1,0:T(8,128)(2,1)S(1)} %get-tuple-element.35), channel_id=1, source_target_pairs={{0,192},{64,0},{128,64},{192,128},{1,193},{65,1},{129,65},{193,129... | collective-permute-start | bytes 442376 | tf_op jit(solution)/shard_map/ppermute | solution.py:66
  48.7 2.3 %shard_map.75 = (bf16[16,1536]{1,0:T(8,128)(2,1)S(1)}, bf16[16,1536]{1,0:T(8,128)(2,1)S(1)}, bf16[16,1536]{1,0:T(8,128)(2,1)S(1)}, bf16[16,1536]{1,0:T(8,128)(2,1)S(1)}) custom-call(bf16[64,6144]{1,0:T(8,128)(2,1)S(1)} %shard_map.74.refs_0_.refs_1_, bf16[3072,768]{1,0:T(8,128)(2,1)S(1)} %shard_map.68.refs_2_.refs_1_, ...), custom_call_target="tpu_custom_call" | custom-call | tf_op jit(solution)/shard_map/pallas_call | solution.py:81
  51.7 3.7 %collective-permute-done.10.refs_1_ = bf16[48,1536]{1,0:T(8,128)(2,1)S(1)} collective-permute-done((bf16[48,1536]{1,0:T(8,128)(2,1)S(1)}, bf16[48,1536]{1,0:T(8,128)(2,1)S(1)}, u32[]{:S(2)}, u32[]{:S(2)}) %collective-permute-start.10) | collective-permute-done | bytes 147488 | tf_op jit(solution)/shard_map/ppermute | solution.py:66
  55.9 4.2 %collective-permute-done.15.refs_5_ = bf16[16,1536]{1,0:T(8,128)(2,1)S(1)} collective-permute-done((bf16[16,1536]{1,0:T(8,128)(2,1)S(1)}, bf16[16,1536]{1,0:T(8,128)(2,1)S(1)}, u32[]{:S(2)}, u32[]{:S(2)}) %collective-permute-start.15) | collective-permute-done | bytes 49184 | tf_op jit(solution)/shard_map/ppermute | solution.py:66
  61.8 2.1 %collective-permute-start.19 = (bf16[64,768]{1,0:T(8,128)(2,1)S(1)}, bf16[64,768]{1,0:T(8,128)(2,1)S(1)}, u32[]{:S(2)}, u32[]{:S(2)}) collective-permute-start(bf16[64,768]{1,0:T(8,128)(2,1)S(1)} %get-tuple-element.40.refs_0_), channel_id=1, source_target_pairs={{0,192},{64,0},{128,64},{192,128},{1,193},{65,1},{129,65},{193,129... | collective-permute-start | bytes 294920 | tf_op jit(solution)/shard_map/ppermute | solution.py:66
  65.1 3.0 %collective-permute-done.18.refs_1_ = bf16[64,768]{1,0:T(8,128)(2,1)S(1)} collective-permute-done((bf16[64,768]{1,0:T(8,128)(2,1)S(1)}, bf16[64,768]{1,0:T(8,128)(2,1)S(1)}, u32[]{:S(2)}, u32[]{:S(2)}) %collective-permute-start.18) | collective-permute-done | bytes 98336 | tf_op jit(solution)/shard_map/ppermute | solution.py:66
  68.1 2.2 %collective-permute-done.20.refs_3_ = bf16[64,768]{1,0:T(8,128)(2,1)S(1)} collective-permute-done((bf16[64,768]{1,0:T(8,128)(2,1)S(1)}, bf16[64,768]{1,0:T(8,128)(2,1)S(1)}, u32[]{:S(2)}, u32[]{:S(2)}) %collective-permute-start.20) | collective-permute-done | bytes 98336 | tf_op jit(solution)/shard_map/ppermute | solution.py:66
  72.3 1.7 %collective-permute-start.22 = (bf16[64,3072]{1,0:T(8,128)(2,1)S(1)}, bf16[64,3072]{1,0:T(8,128)(2,1)S(1)}, u32[]{:S(2)}, u32[]{:S(2)}) collective-permute-start(bf16[64,3072]{1,0:T(8,128)(2,1)S(1)} %get-tuple-element.45.refs_1_.refs_2_), channel_id=1, source_target_pairs={{0,2},{1,9},{2,4},{3,11},{4,6},{5,13},{6,0},{7,15},{8,10},{9,17},{... | collective-permute-start | bytes 1179656 | tf_op jit(solution)/shard_map/ppermute | solution.py:38
  74.0 2.1 %collective-permute-start.23 = (bf16[64,3072]{1,0:T(8,128)(2,1)S(1)}, bf16[64,3072]{1,0:T(8,128)(2,1)S(1)}, u32[]{:S(2)}, u32[]{:S(2)}) collective-permute-start(bf16[64,3072]{1,0:T(8,128)(2,1)S(1)} %get-tuple-element.46), channel_id=1, source_target_pairs={{0,6},{1,25},{2,0},{3,27},{4,2},{5,29},{6,4},{7,31},{8,14},{9,1},{... | collective-permute-start | bytes 1179656 | tf_op jit(solution)/shard_map/ppermute | solution.py:38
  76.1 2.0 %collective-permute-start.24 = (bf16[64,3072]{1,0:T(8,128)(2,1)S(1)}, bf16[64,3072]{1,0:T(8,128)(2,1)S(1)}, u32[]{:S(2)}, u32[]{:S(2)}) collective-permute-start(bf16[64,3072]{1,0:T(8,128)(2,1)S(1)} %get-tuple-element.47), channel_id=1, source_target_pairs={{0,4},{1,17},{2,6},{3,19},{4,0},{5,21},{6,2},{7,23},{8,12},{9,25},... | collective-permute-start | bytes 1179656 | tf_op jit(solution)/shard_map/ppermute | solution.py:38
  82.9 2.3 %collective-permute-start.33 = (bf16[128,384]{1,0:T(8,128)(2,1)S(1)}, bf16[128,384]{1,0:T(8,128)(2,1)S(1)}, u32[]{:S(2)}, u32[]{:S(2)}) collective-permute-start(bf16[128,384]{1,0:T(8,128)(2,1)S(1)} %shard_map.85.refs_0_), channel_id=1, source_target_pairs={{0,64},{64,128},{128,192},{192,0},{1,65},{65,129},{129,193},{193,1... | collective-permute-start | bytes 294920 | tf_op jit(solution)/shard_map/ppermute | solution.py:66
  85.2 2.8 %collective-permute-done.24.refs_3_ = bf16[64,3072]{1,0:T(8,128)(2,1)S(1)} collective-permute-done((bf16[64,3072]{1,0:T(8,128)(2,1)S(1)}, bf16[64,3072]{1,0:T(8,128)(2,1)S(1)}, u32[]{:S(2)}, u32[]{:S(2)}) %collective-permute-start.24) | collective-permute-done | bytes 393248 | tf_op jit(solution)/shard_map/ppermute | solution.py:38
  91.0 3.5 %collective-permute-done.27.refs_1_ = bf16[16,3072]{1,0:T(8,128)(2,1)S(1)} collective-permute-done((bf16[16,3072]{1,0:T(8,128)(2,1)S(1)}, bf16[16,3072]{1,0:T(8,128)(2,1)S(1)}, u32[]{:S(2)}, u32[]{:S(2)}) %collective-permute-start.27) | collective-permute-done | bytes 98336 | tf_op jit(solution)/shard_map/ppermute | solution.py:38
  96.3 2.8 %collective-permute-done.29.refs_3_ = bf16[16,3072]{1,0:T(8,128)(2,1)S(1)} collective-permute-done((bf16[16,3072]{1,0:T(8,128)(2,1)S(1)}, bf16[16,3072]{1,0:T(8,128)(2,1)S(1)}, u32[]{:S(2)}, u32[]{:S(2)}) %collective-permute-start.29) | collective-permute-done | bytes 98336 | tf_op jit(solution)/shard_map/ppermute | solution.py:38
  99.2 6.1 %collective-permute-start.30 = (bf16[8,3072]{1,0:T(8,128)(2,1)S(1)}, bf16[8,3072]{1,0:T(8,128)(2,1)S(1)}, u32[]{:S(2)}, u32[]{:S(2)}) collective-permute-start(bf16[8,3072]{1,0:T(8,128)(2,1)S(1)} %get-tuple-element.54.refs_4_), channel_id=1, source_target_pairs={{0,32},{1,33},{2,34},{3,35},{4,36},{5,37},{6,38},{7,39},{8,40},{9,... | collective-permute-start | bytes 147464 | tf_op jit(solution)/shard_map/ppermute | solution.py:38
  106.2 2.2 %add_convert_fusion = bf16[384,3072]{1,0:T(8,128)(2,1)} fusion(f32[384,3072]{1,0:T(8,128)S(1)} %fusion, bf16[256,6144]{1,0:T(8,128)(2,1)S(1)} %shard_map.81, bf16[512,384]{1,0:T(8,128)(2,1)S(1)} %shard_map.86), kind=kOutput, calls=%fused_computation | convolution fusion | flops 606339072 | bytes 8847360 | tf_op jit(solution)/shard_map/dot_general | solution.py:25
  (80 shorter events, 34.4 us)
Async XLA Ops:
  0.6 9.6 %collective-permute-start.1 = (bf16[3072,384]{1,0:T(8,128)(2,1)}, bf16[3072,384]{1,0:T(8,128)(2,1)S(1)}, u32[]{:S(2)}, u32[]{:S(2)}) collective-permute-start(bf16[3072,384]{1,0:T(8,128)(2,1)} %refs_0_.4), channel_id=1, source_target_pairs={{0,1},{1,0},{2,3},{3,2},{4,5},{5,4},{6,7},{7,6},{8,9},{9,8},{10,11... | collective-permute-start | bytes 7077896 | tf_op jit(solution)/shard_map/ppermute | solution.py:38
  0.7 11.6 %collective-permute-start.2 = (bf16[384,3072]{1,0:T(8,128)(2,1)}, bf16[384,3072]{1,0:T(8,128)(2,1)S(1)}, u32[]{:S(2)}, u32[]{:S(2)}) collective-permute-start(bf16[384,3072]{1,0:T(8,128)(2,1)} %refs_0_.5), channel_id=1, source_target_pairs={{0,1},{1,0},{2,3},{3,2},{4,5},{5,4},{6,7},{7,6},{8,9},{9,8},{10,11... | collective-permute-start | bytes 7077896 | tf_op jit(solution)/shard_map/ppermute | solution.py:38
  2.9 10.9 %collective-permute-start = (bf16[8,6144]{1,0:T(8,128)(2,1)S(1)}, bf16[8,6144]{1,0:T(8,128)(2,1)S(1)}, u32[]{:S(2)}, u32[]{:S(2)}) collective-permute-start(bf16[8,6144]{1,0:T(8,128)(2,1)S(1)} %shard_map.67.refs_0_), channel_id=1, source_target_pairs={{0,32},{1,33},{2,34},{3,35},{4,36},{5,37},{6,38},{7,39},{8,40},{9,... | collective-permute-start | bytes 294920 | tf_op jit(solution)/shard_map/ppermute | solution.py:38
  25.2 7.9 %collective-permute-start.6 = (bf16[32,6144]{1,0:T(8,128)(2,1)S(1)}, bf16[32,6144]{1,0:T(8,128)(2,1)S(1)}, u32[]{:S(2)}, u32[]{:S(2)}) collective-permute-start(bf16[32,6144]{1,0:T(8,128)(2,1)S(1)} %get-tuple-element.30), channel_id=1, source_target_pairs={{0,6},{1,25},{2,0},{3,27},{4,2},{5,29},{6,4},{7,31},{8,14},{9,1},{... | collective-permute-start | bytes 1179656 | tf_op jit(solution)/shard_map/ppermute | solution.py:38
  25.9 8.5 %collective-permute-start.9 = (bf16[32,6144]{1,0:T(8,128)(2,1)S(1)}, bf16[32,6144]{1,0:T(8,128)(2,1)S(1)}, u32[]{:S(2)}, u32[]{:S(2)}) collective-permute-start(bf16[32,6144]{1,0:T(8,128)(2,1)S(1)} %get-tuple-element.31), channel_id=1, source_target_pairs={{0,2},{1,9},{2,4},{3,11},{4,6},{5,13},{6,0},{7,15},{8,10},{9,17},{... | collective-permute-start | bytes 1179656 | tf_op jit(solution)/shard_map/ppermute | solution.py:38
  27.3 10.0 %collective-permute-start.7 = (bf16[32,6144]{1,0:T(8,128)(2,1)S(1)}, bf16[32,6144]{1,0:T(8,128)(2,1)S(1)}, u32[]{:S(2)}, u32[]{:S(2)}) collective-permute-start(bf16[32,6144]{1,0:T(8,128)(2,1)S(1)} %get-tuple-element.31), channel_id=1, source_target_pairs={{0,6},{1,25},{2,0},{3,27},{4,2},{5,29},{6,4},{7,31},{8,14},{9,1},{... | collective-permute-start | bytes 1179656 | tf_op jit(solution)/shard_map/ppermute | solution.py:38
  28.6 10.0 %collective-permute-start.8 = (bf16[32,6144]{1,0:T(8,128)(2,1)S(1)}, bf16[32,6144]{1,0:T(8,128)(2,1)S(1)}, u32[]{:S(2)}, u32[]{:S(2)}) collective-permute-start(bf16[32,6144]{1,0:T(8,128)(2,1)S(1)} %get-tuple-element.30), channel_id=1, source_target_pairs={{0,2},{1,9},{2,4},{3,11},{4,6},{5,13},{6,0},{7,15},{8,10},{9,17},{... | collective-permute-start | bytes 1179656 | tf_op jit(solution)/shard_map/ppermute | solution.py:38
  33.1 15.5 %collective-permute-start.13 = (bf16[32,6144]{1,0:T(8,128)(2,1)S(1)}, bf16[32,6144]{1,0:T(8,128)(2,1)S(1)}, u32[]{:S(2)}, u32[]{:S(2)}) collective-permute-start(bf16[32,6144]{1,0:T(8,128)(2,1)S(1)} %collective-permute-done.6.refs_1_), channel_id=1, source_target_pairs={{0,6},{1,25},{2,0},{3,27},{4,2},{5,29},{6,4},{7,31},{8,14},{9,1},{... | collective-permute-start | bytes 1179656 | tf_op jit(solution)/shard_map/ppermute | solution.py:38
  34.4 14.3 %collective-permute-start.14 = (bf16[32,6144]{1,0:T(8,128)(2,1)S(1)}, bf16[32,6144]{1,0:T(8,128)(2,1)S(1)}, u32[]{:S(2)}, u32[]{:S(2)}) collective-permute-start(bf16[32,6144]{1,0:T(8,128)(2,1)S(1)} %collective-permute-done.9.refs_4_), channel_id=1, source_target_pairs={{0,2},{1,9},{2,4},{3,11},{4,6},{5,13},{6,0},{7,15},{8,10},{9,17},{... | collective-permute-start | bytes 1179656 | tf_op jit(solution)/shard_map/ppermute | solution.py:38
  41.3 14.0 %collective-permute-start.10 = (bf16[48,1536]{1,0:T(8,128)(2,1)S(1)}, bf16[48,1536]{1,0:T(8,128)(2,1)S(1)}, u32[]{:S(2)}, u32[]{:S(2)}) collective-permute-start(bf16[48,1536]{1,0:T(8,128)(2,1)S(1)} %get-tuple-element.33), channel_id=1, source_target_pairs={{0,128},{64,192},{128,0},{192,64},{1,129},{65,193},{129,1},{193,65... | collective-permute-start | bytes 442376 | tf_op jit(solution)/shard_map/ppermute | solution.py:66
  44.8 11.1 %collective-permute-start.11 = (bf16[48,1536]{1,0:T(8,128)(2,1)S(1)}, bf16[48,1536]{1,0:T(8,128)(2,1)S(1)}, u32[]{:S(2)}, u32[]{:S(2)}) collective-permute-start(bf16[48,1536]{1,0:T(8,128)(2,1)S(1)} %get-tuple-element.34), channel_id=1, source_target_pairs={{0,64},{64,128},{128,192},{192,0},{1,65},{65,129},{129,193},{193,1... | collective-permute-start | bytes 442376 | tf_op jit(solution)/shard_map/ppermute | solution.py:66
  44.8 11.1 %collective-permute-start.12 = (bf16[48,1536]{1,0:T(8,128)(2,1)S(1)}, bf16[48,1536]{1,0:T(8,128)(2,1)S(1)}, u32[]{:S(2)}, u32[]{:S(2)}) collective-permute-start(bf16[48,1536]{1,0:T(8,128)(2,1)S(1)} %get-tuple-element.35), channel_id=1, source_target_pairs={{0,192},{64,0},{128,64},{192,128},{1,193},{65,1},{129,65},{193,129... | collective-permute-start | bytes 442376 | tf_op jit(solution)/shard_map/ppermute | solution.py:66
  51.0 9.1 %collective-permute-start.15 = (bf16[16,1536]{1,0:T(8,128)(2,1)S(1)}, bf16[16,1536]{1,0:T(8,128)(2,1)S(1)}, u32[]{:S(2)}, u32[]{:S(2)}) collective-permute-start(bf16[16,1536]{1,0:T(8,128)(2,1)S(1)} %get-tuple-element.37), channel_id=1, source_target_pairs={{0,128},{64,192},{128,0},{192,64},{1,129},{65,193},{129,1},{193,65... | collective-permute-start | bytes 147464 | tf_op jit(solution)/shard_map/ppermute | solution.py:66
  51.1 9.0 %collective-permute-start.16 = (bf16[16,1536]{1,0:T(8,128)(2,1)S(1)}, bf16[16,1536]{1,0:T(8,128)(2,1)S(1)}, u32[]{:S(2)}, u32[]{:S(2)}) collective-permute-start(bf16[16,1536]{1,0:T(8,128)(2,1)S(1)} %get-tuple-element.38), channel_id=1, source_target_pairs={{0,64},{64,128},{128,192},{192,0},{1,65},{65,129},{129,193},{193,1... | collective-permute-start | bytes 147464 | tf_op jit(solution)/shard_map/ppermute | solution.py:66
  60.3 7.8 %collective-permute-start.18 = (bf16[64,768]{1,0:T(8,128)(2,1)S(1)}, bf16[64,768]{1,0:T(8,128)(2,1)S(1)}, u32[]{:S(2)}, u32[]{:S(2)}) collective-permute-start(bf16[64,768]{1,0:T(8,128)(2,1)S(1)} %get-tuple-element.40.refs_0_), channel_id=1, source_target_pairs={{0,128},{64,192},{128,0},{192,64},{1,129},{65,193},{129,1},{193,65... | collective-permute-start | bytes 294920 | tf_op jit(solution)/shard_map/ppermute | solution.py:66
  72.2 15.8 %collective-permute-start.26 = (bf16[256,6144]{1,0:T(8,128)(2,1)S(1)}, bf16[256,6144]{1,0:T(8,128)(2,1)S(1)}, u32[]{:S(2)}, u32[]{:S(2)}) collective-permute-start(bf16[256,6144]{1,0:T(8,128)(2,1)S(1)} %shard_map.81), channel_id=1, source_target_pairs={{0,1},{1,0},{2,3},{3,2},{4,5},{5,4},{6,7},{7,6},{8,9},{9,8},{10,11... | collective-permute-start | bytes 9437192 | tf_op jit(solution)/shard_map/ppermute | solution.py:38
  72.3 9.4 %collective-permute-start.22 = (bf16[64,3072]{1,0:T(8,128)(2,1)S(1)}, bf16[64,3072]{1,0:T(8,128)(2,1)S(1)}, u32[]{:S(2)}, u32[]{:S(2)}) collective-permute-start(bf16[64,3072]{1,0:T(8,128)(2,1)S(1)} %get-tuple-element.45.refs_1_.refs_2_), channel_id=1, source_target_pairs={{0,2},{1,9},{2,4},{3,11},{4,6},{5,13},{6,0},{7,15},{8,10},{9,17},{... | collective-permute-start | bytes 1179656 | tf_op jit(solution)/shard_map/ppermute | solution.py:38
  74.0 8.9 %collective-permute-start.23 = (bf16[64,3072]{1,0:T(8,128)(2,1)S(1)}, bf16[64,3072]{1,0:T(8,128)(2,1)S(1)}, u32[]{:S(2)}, u32[]{:S(2)}) collective-permute-start(bf16[64,3072]{1,0:T(8,128)(2,1)S(1)} %get-tuple-element.46), channel_id=1, source_target_pairs={{0,6},{1,25},{2,0},{3,27},{4,2},{5,29},{6,4},{7,31},{8,14},{9,1},{... | collective-permute-start | bytes 1179656 | tf_op jit(solution)/shard_map/ppermute | solution.py:38
  76.1 11.9 %collective-permute-start.24 = (bf16[64,3072]{1,0:T(8,128)(2,1)S(1)}, bf16[64,3072]{1,0:T(8,128)(2,1)S(1)}, u32[]{:S(2)}, u32[]{:S(2)}) collective-permute-start(bf16[64,3072]{1,0:T(8,128)(2,1)S(1)} %get-tuple-element.47), channel_id=1, source_target_pairs={{0,4},{1,17},{2,6},{3,19},{4,0},{5,21},{6,2},{7,23},{8,12},{9,25},... | collective-permute-start | bytes 1179656 | tf_op jit(solution)/shard_map/ppermute | solution.py:38
  79.8 25.5 %collective-permute-start.31 = (bf16[128,384]{1,0:T(8,128)(2,1)S(1)}, bf16[128,384]{1,0:T(8,128)(2,1)S(1)}, u32[]{:S(2)}, u32[]{:S(2)}) collective-permute-start(bf16[128,384]{1,0:T(8,128)(2,1)S(1)} %shard_map.85.refs_0_), channel_id=1, source_target_pairs={{0,128},{64,192},{128,0},{192,64},{1,129},{65,193},{129,1},{193,65... | collective-permute-start | bytes 294920 | tf_op jit(solution)/shard_map/ppermute | solution.py:66
  81.8 23.6 %collective-permute-start.32 = (bf16[128,384]{1,0:T(8,128)(2,1)S(1)}, bf16[128,384]{1,0:T(8,128)(2,1)S(1)}, u32[]{:S(2)}, u32[]{:S(2)}) collective-permute-start(bf16[128,384]{1,0:T(8,128)(2,1)S(1)} %shard_map.85.refs_0_), channel_id=1, source_target_pairs={{0,192},{64,0},{128,64},{192,128},{1,193},{65,1},{129,65},{193,129... | collective-permute-start | bytes 294920 | tf_op jit(solution)/shard_map/ppermute | solution.py:66
  82.9 22.5 %collective-permute-start.33 = (bf16[128,384]{1,0:T(8,128)(2,1)S(1)}, bf16[128,384]{1,0:T(8,128)(2,1)S(1)}, u32[]{:S(2)}, u32[]{:S(2)}) collective-permute-start(bf16[128,384]{1,0:T(8,128)(2,1)S(1)} %shard_map.85.refs_0_), channel_id=1, source_target_pairs={{0,64},{64,128},{128,192},{192,0},{1,65},{65,129},{129,193},{193,1... | collective-permute-start | bytes 294920 | tf_op jit(solution)/shard_map/ppermute | solution.py:66
  88.3 8.0 %collective-permute-start.28 = (bf16[16,3072]{1,0:T(8,128)(2,1)S(1)}, bf16[16,3072]{1,0:T(8,128)(2,1)S(1)}, u32[]{:S(2)}, u32[]{:S(2)}) collective-permute-start(bf16[16,3072]{1,0:T(8,128)(2,1)S(1)} %get-tuple-element.51), channel_id=1, source_target_pairs={{0,8},{1,3},{2,10},{3,5},{4,12},{5,7},{6,14},{7,1},{8,16},{9,11},{... | collective-permute-start | bytes 294920 | tf_op jit(solution)/shard_map/ppermute | solution.py:38
  99.2 9.3 %collective-permute-start.30 = (bf16[8,3072]{1,0:T(8,128)(2,1)S(1)}, bf16[8,3072]{1,0:T(8,128)(2,1)S(1)}, u32[]{:S(2)}, u32[]{:S(2)}) collective-permute-start(bf16[8,3072]{1,0:T(8,128)(2,1)S(1)} %get-tuple-element.54.refs_4_), channel_id=1, source_target_pairs={{0,32},{1,33},{2,34},{3,35},{4,36},{5,37},{6,38},{7,39},{8,40},{9,... | collective-permute-start | bytes 147464 | tf_op jit(solution)/shard_map/ppermute | solution.py:38
  (15 other events, 66.8 us)
